TPU v7x, 256 devices: a whole 4x4x8 slice. The times are simulated.
256 devices in a mesh: ctx: 32 (over z, y), tp: 8 (over x, core).
Axes of the slice: x: 4, y: 4, z: 8, core: 2. Of those that a mesh axis runs over, the one named last changes fastest.
Arguments:
- inputs: bfloat16 [8192, 16384], P('ctx', 'tp'), may hold values from -11 to 11
- gate_input: bfloat16 [8192, 16384], P('ctx', 'tp'), may hold values from -6 to 6
- write_proj: bfloat16 [8192, 1024], P('ctx', 'tp'), may hold values from -6 to 6
- read_proj: bfloat16 [8192, 1024], P('ctx', 'tp'), may hold values from -0.5 to 0.5
- step_raw: float32 [256, 8192], P('tp', 'ctx'), may hold values from -1.2 to 1.2
- step_bias: float32 [256], P('tp'), may hold values from -3.3 to -0.1
- decay_log: float32 [256], P('tp')
- skip_gain: float32 [256], P('tp'), may hold values from 0.5 to 1.5
- norm_gain: float32 [16384], P('tp'), may hold values from 0.5 to 1.5
- start_state: float32 [8, 32, 8192], P('tp', 'ctx'), may hold values from -18 to 18
- out_grad: bfloat16 [8192, 16384], P('ctx', 'tp'), may hold values from -11 to 11
Outputs:
- output: bfloat16 [8192, 16384], P('ctx', 'tp')
- final_state: float32 [8, 32, 8192], P('tp', 'ctx')
- grad_inputs: bfloat16 [8192, 16384], P('ctx', 'tp')
- grad_gate: bfloat16 [8192, 16384], P('ctx', 'tp')
- grad_write: bfloat16 [8192, 1024], P('ctx', 'tp')
- grad_read: bfloat16 [8192, 1024], P('ctx', 'tp')
- grad_step: float32 [256, 8192], P('tp', 'ctx')
- grad_heads: float32 [3, 256], P(None, 'tp')
- grad_norm: float32 [16384], P('tp')
All inputs are finite; a program needn't handle non-finite values.
Results may differ from a plain program's by a relative error of at most 0.014.
Values sent between devices are 32-bit elements; how exact they have to be, the bound alone decides.
A program may use at most 128 MiB of HBM per device.

v0:
```python
import math

import jax
import jax.numpy as jnp
from jax import lax
from jax.sharding import PartitionSpec as P

P_SIZE = 64
N = 128
STRETCH = 256
INNER = 16384


eps_norm = 1e-05


def carried_in(part, axis, combine, identity, reverse):
    count = lax.axis_size(axis)
    place = lax.axis_index(axis)
    ahead = count - 1 - place if reverse else place
    gathered = jax.tree.map(lambda a: lax.all_gather(a, axis), part)
    state = jax.tree.map(lambda a, e: jnp.zeros_like(a) + jnp.asarray(e, a.dtype), part, identity)

    def one(hop, state):
        source = count - 1 - hop if reverse else hop
        return combine(
            state, jax.tree.map(lambda a: lax.dynamic_index_in_dim(a, source, 0, False), gathered)
        )

    return lax.fori_loop(0, ahead, one, state)


def spread(value, axis, root):
    mine = lax.axis_index(axis) == root
    return lax.psum(jnp.where(mine, value, jnp.zeros_like(value)), axis)


def local_parts(inputs, write_proj, read_proj, step_raw, step_bias, decay_log):
    blocks = inputs.shape[0] // STRETCH
    groups = write_proj.shape[1] // N
    head_count = step_raw.shape[0]
    per_group = head_count // groups
    input_blocks = inputs.reshape(blocks, STRETCH, groups, per_group, P_SIZE)
    write_blocks = write_proj.reshape(blocks, STRETCH, groups, N)
    read_blocks = read_proj.reshape(blocks, STRETCH, groups, N)
    step_size = jax.nn.softplus(step_raw + step_bias[:, None]).reshape(
        groups, per_group, blocks, STRETCH
    )
    decay_rate = jnp.exp(decay_log).reshape(groups, per_group, 1, 1)
    cumulative = jnp.cumsum(-decay_rate * step_size, axis=3)
    read_write = jnp.einsum(
        "kign,kjgn->gkij", read_blocks, write_blocks, preferred_element_type=jnp.float32
    )
    log_gap = cumulative[..., :, None] - cumulative[..., None, :]
    causal = jnp.arange(STRETCH)[:, None] >= jnp.arange(STRETCH)[None, :]
    decay_matrix = jnp.exp(jnp.where(causal, log_gap, -1e30))
    mixing = (read_write[:, None] * decay_matrix * step_size[..., None, :]).astype(jnp.bfloat16)
    y_intra = jnp.einsum(
        "ghkij,kjghp->kighp", mixing, input_blocks, preferred_element_type=jnp.float32
    )
    to_end = jnp.exp(cumulative[..., -1:] - cumulative) * step_size
    write_scaled = (to_end[..., None] * jnp.moveaxis(write_blocks, 2, 0)[:, None]).astype(
        jnp.bfloat16
    )
    stretch_states = jnp.einsum(
        "ghkjn,kjghp->ghkpn", write_scaled, input_blocks, preferred_element_type=jnp.float32
    )
    return (y_intra, stretch_states, cumulative)


def read_states(read_proj, cumulative, incoming):
    blocks = read_proj.shape[0] // STRETCH
    groups = incoming.shape[0]
    read_blocks = read_proj.reshape(blocks, STRETCH, groups, N)
    rounded = incoming.astype(jnp.bfloat16)
    product = jnp.einsum(
        "kign,ghkpn->kighp", read_blocks, rounded, preferred_element_type=jnp.float32
    )
    return product * jnp.exp(jnp.transpose(cumulative, (2, 3, 0, 1)))[..., None]


def compose(first_part, second_part):
    return (
        first_part[0] + second_part[0],
        jnp.exp(second_part[0])[..., None] * first_part[1] + second_part[1],
    )


def advance(running, element):
    return (jnp.exp(element[1])[..., None, None] * running + element[0], running)


def retreat(running, element):
    return (element[0] + jnp.exp(element[1])[..., None, None] * running, running)


def on_device(
    inputs,
    gate_input,
    write_proj,
    read_proj,
    step_raw,
    step_bias,
    decay_log,
    skip_gain,
    norm_gain,
    start_state,
    out_grad,
):
    tok_rows = inputs.shape[0]
    groups = write_proj.shape[1] // N
    head_count = step_raw.shape[0]
    per_group = head_count // groups
    state_width = P_SIZE * N
    owned_heads = start_state.shape[1]
    (y_intra, stretch_states, cumulative), parts_pullback = jax.vjp(
        local_parts, inputs, write_proj, read_proj, step_raw, step_bias, decay_log
    )
    end_logs = cumulative[..., -1]
    zero_state = jnp.zeros((groups, per_group, P_SIZE, N), jnp.float32)
    last_zero, start_zero = lax.scan(
        advance, zero_state, (jnp.moveaxis(stretch_states, 2, 0), jnp.moveaxis(end_logs, 2, 0))
    )
    start_zero = jnp.moveaxis(start_zero, 0, 2)
    log_total = jnp.sum(end_logs, axis=2)
    flat_last = last_zero.reshape(groups, per_group, state_width)
    identity = (jnp.zeros_like(log_total), jnp.zeros_like(flat_last))
    before_pair = carried_in((log_total, flat_last), "ctx", compose, identity, False)
    starts = lax.all_gather(start_state, "ctx", axis=1, tiled=True)
    state_in = jnp.exp(before_pair[0])[..., None] * starts + before_pair[1]
    device_out = jnp.exp(log_total)[..., None] * state_in + flat_last
    last_out = spread(device_out, "ctx", lax.axis_size("ctx") - 1)
    final_state = lax.dynamic_slice_in_dim(
        last_out, lax.axis_index("ctx") * owned_heads, owned_heads, 1
    )
    before_log = jnp.cumsum(end_logs, axis=2) - end_logs
    incoming = start_zero + jnp.exp(before_log)[..., None, None] * state_in.reshape(
        groups, per_group, 1, P_SIZE, N
    )
    y_inter, read_pullback = jax.vjp(read_states, read_proj, cumulative, incoming)
    skip_cols = jnp.repeat(skip_gain, P_SIZE)
    ssd_out = (y_intra + y_inter).reshape(tok_rows, head_count * P_SIZE) + skip_cols * inputs
    gate_float = gate_input.astype(jnp.float32)
    sigmoid_gate = jax.nn.sigmoid(gate_float)
    gate_act = gate_float * sigmoid_gate
    gated_values = ssd_out * gate_act
    square_sum = lax.psum(jnp.sum(gated_values * gated_values, axis=1), "tp")
    inverse = lax.rsqrt(square_sum / INNER + eps_norm)
    output = (gated_values * inverse[:, None] * norm_gain).astype(jnp.bfloat16)
    grad_float = out_grad.astype(jnp.float32)
    scaled_grad = grad_float * norm_gain
    norm_part = jnp.sum(grad_float * gated_values * inverse[:, None], axis=0)
    cross_sum = lax.psum(jnp.sum(scaled_grad * gated_values, axis=1), "tp")
    inverse_cube = inverse * inverse * inverse
    grad_mixed = (
        inverse[:, None] * scaled_grad - gated_values * (inverse_cube * cross_sum / INNER)[:, None]
    )
    grad_ssd = grad_mixed * gate_act
    grad_gate = (
        grad_mixed * ssd_out * sigmoid_gate * (1.0 + gate_float * (1.0 - sigmoid_gate))
    ).astype(jnp.bfloat16)
    skip_part = jnp.sum((grad_ssd * inputs).reshape(tok_rows, head_count, P_SIZE), axis=(0, 2))
    skip_input = (grad_ssd * skip_cols).astype(jnp.bfloat16)
    grad_blocks = grad_ssd.reshape(tok_rows // STRETCH, STRETCH, groups, per_group, P_SIZE)
    read_inter, cum_inter, grad_incoming = read_pullback(grad_blocks)
    device_grad, later_zero = lax.scan(
        retreat,
        zero_state,
        (jnp.moveaxis(grad_incoming, 2, 0), jnp.moveaxis(end_logs, 2, 0)),
        reverse=True,
    )
    later_zero = jnp.moveaxis(later_zero, 0, 2)
    flat_grad = device_grad.reshape(groups, per_group, state_width)
    grad_pair = carried_in(
        (log_total, flat_grad),
        "ctx",
        compose,
        (jnp.zeros_like(log_total), jnp.zeros_like(flat_grad)),
        True,
    )
    grad_out = grad_pair[1]
    after_log = jnp.sum(end_logs, axis=2, keepdims=True) - jnp.cumsum(end_logs, axis=2)
    later_true = later_zero + jnp.exp(after_log)[..., None, None] * grad_out.reshape(
        groups, per_group, 1, P_SIZE, N
    )
    end_grad = jnp.exp(end_logs) * jnp.sum(later_true * incoming, axis=(3, 4))
    cum_grad = cum_inter + jnp.pad(end_grad[..., None], ((0, 0), (0, 0), (0, 0), (STRETCH - 1, 0)))
    grad_in_parts, grad_write, read_parts, grad_step, bias_part, decay_part = parts_pullback(
        (grad_blocks, later_true, cum_grad)
    )
    grad_inputs = grad_in_parts + skip_input
    grad_read = read_parts + read_inter
    totals = lax.psum((norm_part, bias_part, decay_part, skip_part), "ctx")
    grad_scale = 1.0 / math.sqrt(tok_rows * lax.axis_size("ctx"))
    grad_heads = jnp.stack([totals[1], totals[2], totals[3]]) * grad_scale
    grad_norm = totals[0] * grad_scale
    return (
        output,
        final_state,
        grad_inputs,
        grad_gate,
        grad_write,
        grad_read,
        grad_step,
        grad_heads,
        grad_norm,
    )


def solution(mesh):
    in_specs = (
        P("ctx", "tp"),
        P("ctx", "tp"),
        P("ctx", "tp"),
        P("ctx", "tp"),
        P("tp", "ctx"),
        P("tp"),
        P("tp"),
        P("tp"),
        P("tp"),
        P("tp", "ctx", None),
        P("ctx", "tp"),
    )
    out_specs = (
        P("ctx", "tp"),
        P("tp", "ctx", None),
        P("ctx", "tp"),
        P("ctx", "tp"),
        P("ctx", "tp"),
        P("ctx", "tp"),
        P("tp", "ctx"),
        P(None, "tp"),
        P("tp"),
    )
    return jax.shard_map(
        on_device, mesh=mesh, in_specs=in_specs, out_specs=out_specs, check_vma=False
    )
```

profile of v0, /device:TPU:32, one launch (start us, length us, event | category | flops | bytes accessed | tf_op | source)
XLA Modules:
  0.0 866.6 jit_solution(13732812357146565047)
XLA Ops:
  7.9 1.5 compare_select_fusion.2
  11.6 1.5 copy.158
  17.3 40.3 %all-gather = f32[32,32,1,1]{1,3,2,0:T(1,128)S(1)} all-gather(f32[1,32,1,1]{1,3,2,0:T(1,128)S(1)} %copy.161), channel_id=2, replica_groups=mesh['ctx'=32,'tp'=8] {'ctx'}, dimensions={0}, use_global_device_ids=true | all-gather | bytes 4224 | tf_op jit(solution)/shard_map/all_gather | solution.py:21
  58.5 191.8 %all-gather.5.cloned.1.call-done = f32[32,1,32,8192]{3,2,1,0:T(8,128)} async-done(((f32[1,1,32,8192]{3,2,1,0:T(8,128)}), f32[32,1,32,8192]{3,2,1,0:T(8,128)}) %all-gather.5.cloned.1.call-update) | async-done | bytes 33554448 | tf_op jit(solution)/shard_map/all_gather | solution.py:21
  250.3 6.1 while.7
  250.4 1.5 bitcast_add_fusion.15
  251.9 1.5 bitcast_add_fusion.15
  253.4 1.5 bitcast_add_fusion.15
  255.0 1.5 bitcast_add_fusion.15
  256.5 70.5 %all-gather.7.cloned.1.call-done = f32[1,32,8192]{2,0,1:T(1,128)} async-done(((f32[1,1,8192]{2,0,1:T(1,128)}), f32[1,32,8192]{2,0,1:T(1,128)}) %all-gather.7.cloned.1.call-update) | async-done | bytes 1048592 | tf_op jit(solution)/shard_map/all_gather | solution.py:129
  326.9 3.0 add_select_fusion
  331.6 4.1 bitcast_add_fusion.3
  335.7 1.9 copy.165
  337.6 3.7 multiply_reduce_fusion
  341.3 12.4 %psum.49 = f32[256]{0:T(256)S(1)} all-reduce(f32[256]{0:T(256)S(1)} %get-tuple-element.317), channel_id=1, replica_groups=mesh['ctx'=32,'tp'=8] {'tp'}, use_global_device_ids=true, to_apply=%region_5.6 | all-reduce | flops 256 | bytes 2048 | tf_op jit(solution)/shard_map/psum | solution.py:147
  353.8 2.5 fusion.24
  356.3 12.7 %psum.51 = f32[256]{0:T(256)S(1)} all-reduce(f32[256]{0:T(256)S(1)} %get-tuple-element.278), channel_id=1, replica_groups=mesh['ctx'=32,'tp'=8] {'tp'}, use_global_device_ids=true, to_apply=%region_8.9 | all-reduce | flops 256 | bytes 2048 | tf_op jit(solution)/shard_map/psum | solution.py:153
  369.0 5.0 fusion.22
  374.0 1.9 copy.166
  377.4 2.4 reshape.544
  379.8 2.4 broadcast_add_fusion
  383.6 7.9 fusion.8
  393.9 3.7 fusion.44
  397.5 80.6 %all-reduce.5.cloned.1.call-done = f32[1,32,8192]{2,1,0:T(8,128)} async-done(((f32[1,32,8192]{2,1,0:T(8,128)}), f32[1,32,8192]{2,1,0:T(8,128)}) %all-reduce.5.cloned.1.call-update) | async-done | bytes 1048592 | tf_op jit(solution)/shard_map/psum | solution.py:35
  478.1 1.6 constant_dynamic-slice_fusion.1
  479.7 230.7 %all-gather.9.cloned.1.call-done = f32[32,1,32,8192]{3,2,1,0:T(8,128)} async-done(((f32[1,1,32,8192]{3,2,1,0:T(8,128)}), f32[32,1,32,8192]{3,2,1,0:T(8,128)}) %all-gather.9.cloned.1.call-update) | async-done | bytes 33554448 | tf_op jit(solution)/shard_map/all_gather | solution.py:21
  710.5 57.5 %while.8 = (s32[]{:T(128)}, f32[1,32,8192]{2,1,0:T(8,128)S(1)}, s32[]{:T(128)}, f32[32,1,32]{2,1,0:T(1,128)}, f32[32,1,32,8192]{3,2,1,0:T(8,128)}, /*index=5*/s32[]{:T(128)}, s32[]{:T(128)}, s32[]{:T(128)}, s32[]{:T(128)}) while((s32[]{:T(128)}, f32[1,32,8192]{2,1,0:T(8,128)S(1)}, s32[]{:T(128)}, f32[32,1,32]{2,1,0:T(1,128)}, ...), condition=%wide.region_10.11_spmd, body=%wide.region_9.10_spmd.sunk | while | flops 524294 | bytes 3146267 | solution.py:30
  711.1 1.5 bitcast_add_fusion.16
  771.3 2.5 reduce-window.16
  774.0 4.2 fusion.49
  779.2 1.5 copy.168
  783.2 75.7 %all-reduce.2 = (f32[1,32]{1,0:T(1,128)S(1)}, f32[1,32]{1,0:T(1,128)S(1)}, f32[1,32]{1,0:T(1,128)S(1)}, f32[2048]{0:T(1024)S(1)}) all-reduce(f32[1,32]{1,0:T(1,128)S(1)} %bitcast.232, f32[1,32]{1,0:T(1,128)S(1)} %multiply_bitcast_fusion, f32[1,32]{1,0:T(1,128)S(1)} %bitcast.230, ...), channel_id=1, replica_groups=mesh['ctx'=32,'tp'=8] {'ctx'}, use_global_device_ids=true, to_apply=%region_28.29 | all-reduce | flops 2144 | bytes 17152 | tf_op jit(solution)/shard_map/psum | solution.py:193
  (216 shorter events, 78.1 us)
Async XLA Ops:
  7.2 50.4 %copy-start = (bf16[256,128]{1,0:T(8,128)(2,1)S(1)}, bf16[256,128]{1,0:T(8,128)(2,1)}, u32[]{:S(2)}) copy-start(bf16[256,128]{1,0:T(8,128)(2,1)} %param.18) | copy-start | bytes 196612
  7.2 6.0 copy-start.29
  7.2 6.0 copy-start.10
  7.2 243.0 %all-gather.5.cloned.1.call-start = ((), (), s32[]{:S(2)}) async-start(), calls=%async_computation | async-start | bytes 34603008 | tf_op jit(solution)/shard_map/all_gather | solution.py:21
  7.9 2.3 copy-start.37
  10.8 6.0 copy-start.32
  11.6 3.1 copy-start.13
  13.2 2.8 copy-start.6
  13.3 2.6 copy-start.20
  15.9 41.7 %copy-start.9 = (bf16[256,128]{1,0:T(8,128)(2,1)S(1)}, bf16[256,128]{1,0:T(8,128)(2,1)}, u32[]{:S(2)}) copy-start(bf16[256,128]{1,0:T(8,128)(2,1)} %param.17) | copy-start | bytes 196612
  15.9 311.0 %all-gather.7.cloned.1.call-start = ((), (), s32[]{:S(2)}) async-start(), calls=%async_computation.1 | async-start | bytes 1081344 | tf_op jit(solution)/shard_map/all_gather | solution.py:129
  16.7 461.4 %all-reduce.5.cloned.1.call-start = ((), (), s32[]{:S(2)}) async-start(), calls=%async_computation.2 | async-start | bytes 2097152 | tf_op jit(solution)/shard_map/psum | solution.py:35
  16.8 314.7 %copy-start.18 = (pred[256,256]{1,0:T(8,128)(4,1)}, pred[256,256]{1,0:T(8,128)(4,1)S(1)}, u32[]{:S(2)}) copy-start(pred[256,256]{1,0:T(8,128)(4,1)S(1)} %iota_compare_fusion) | copy-start | bytes 196612
  16.8 313.2 %copy-start.35 = (f32[32]{0:T(128)}, f32[32]{0:T(128)S(1)}, u32[]{:S(2)}) copy-start(f32[32]{0:T(128)S(1)} %get-tuple-element.329) | copy-start | bytes 388
  256.4 73.5 %copy-start.28 = (f32[32,1,32]{2,1,0:T(1,128)}, f32[32,1,32]{2,1,0:T(1,128)S(1)}, u32[]{:S(2)}) copy-start(f32[32,1,32]{2,1,0:T(1,128)S(1)} %get-tuple-element.470) | copy-start | bytes 12292
  329.9 380.5 %all-gather.9.cloned.1.call-start = ((), (), s32[]{:S(2)}) async-start(), calls=%async_computation.3 | async-start | bytes 34603008 | tf_op jit(solution)/shard_map/all_gather | solution.py:21
  330.2 1.4 copy-start.11
  331.5 4.2 copy-start.2
  337.6 16.2 %copy-start.27 = (f32[2048]{0:T(1024)S(1)}, f32[2048]{0:T(1024)}, u32[]{:S(2)}) copy-start(f32[2048]{0:T(1024)} %param.23) | copy-start | bytes 24580
  383.6 8.1 copy-start.3
  710.5 57.6 %copy-start.36 = (f32[32]{0:T(128)S(1)}, f32[32]{0:T(128)}, u32[]{:S(2)}) copy-start(f32[32]{0:T(128)} %copy-done.35) | copy-start | bytes 388
  769.6 1.6 copy-start.25
  769.6 1.6 copy-start.26
  769.6 4.3 copy-start.14
  773.9 6.7 copy-start.1
  780.7 1.6 copy-start.17
  780.7 1.6 copy-start.24
  780.7 1.6 copy-start.31
  780.7 1.6 copy-start.34
  780.7 1.6 copy-start.38
  780.7 2.4 copy-start.41
  780.7 2.4 copy-start.39
  (14 other events, 15.5 us)
Sparse Core Ops, SparseCore 0:
  16.1 234.1 all-gather.4
  252.8 74.0 all-gather.6
  331.0 147.0 all-reduce.4
  480.5 229.8 all-gather.8
where the time goes:
time: 876 us; the launch traced here: 867 us
  waiting for transfers between devices  574 us (66%)
  blocking collectives  141 us (16%)
  other arithmetic  74 us (8%)
  local copies, waits for them, and re-layouts  34.7 us (4%)
  matrix products  27.1 us (3%)
  between operations  14.5 us (2%)
    all_gather x2, waiting for transfers between devices, carried_in(): gathered = jax.tree.map(lambda a: lax.all_gather(a, axis), part)  422 us
    psum x1, waiting for transfers between devices, spread(): return lax.psum(jnp.where(mine, value, jnp.zeros_like(value)), axis)  80.6 us
    psum x1, blocking collectives, on_device(): totals = lax.psum((norm_part, bias_part, decay_part, skip_part), 'ctx')  75.7 us
    all_gather x1, waiting for transfers between devices, on_device(): starts = lax.all_gather(start_state, 'ctx', axis=1, tiled=True)  70.5 us
    add x31, other arithmetic, compose(): jnp.exp(second_part[0])[..., None] * first_part[1] + second_part[1]  45.4 us
    all_gather x1, blocking collectives, carried_in(): gathered = jax.tree.map(lambda a: lax.all_gather(a, axis), part)  40.3 us
  transfers between devices with their start and end apart: 4, of which 4 were waited for; matrix products, arithmetic and copies ran while one was open for 6% of the time, Pallas kernels for 0%

commit v1 on v0

v1 whole, which is shorter than its diff:
```python
import functools
import math

import jax
import jax.numpy as jnp
from jax import lax
from jax.experimental import pallas as pl
from jax.experimental.pallas import tpu as pltpu
from jax.sharding import PartitionSpec as P

P_SIZE = 64
N = 128
NY = 4
EPS = 1e-05
F32 = jnp.float32
BF = jnp.bfloat16
MESH = pl.DeviceIdType.MESH


def contract(a, b, da, db):
    return lax.dot_general(a, b, (((da,), (db,)), ((), ())), preferred_element_type=F32)


def nn(a, b):
    return contract(a, b, 1, 0)


def nt(a, b):
    return contract(a, b, 1, 1)


def tn(a, b):
    return contract(a, b, 0, 0)


def split3(a):
    hi = a.astype(BF)
    rest = a - hi.astype(F32)
    mid = rest.astype(BF)
    return hi, mid, (rest - mid.astype(F32)).astype(BF)


def nn3(a, b):
    hi, mid, lo = split3(a)
    return nn(hi, b) + (nn(mid, b) + nn(lo, b))


def iota(shape, dim):
    return lax.broadcasted_iota(jnp.int32, shape, dim)


def kernel(
    ny,
    nz,
    ntp,
    x_ref,
    g_ref,
    w_ref,
    r_ref,
    raw_ref,
    bias_ref,
    decay_ref,
    skip_ref,
    gain_ref,
    start_ref,
    og_ref,
    out_ref,
    fin_ref,
    dx_ref,
    dg_ref,
    dw_ref,
    dr_ref,
    dstep_ref,
    dheads_ref,
    dnorm_ref,
    st_hi,
    st_mid,
    lhs_ref,
    rhs_ref,
    ahl_ref,
    dl_row,
    te_ref,
    e_ref,
    dl_ref,
    xs_ref,
    ssd_ref,
    sig_ref,
    v_ref,
    d_ref,
    de_ref,
    dxi_ref,
    rwm_ref,
    rwt_ref,
    drwt_ref,
    acc_ref,
    invk_ref,
    rk_ref,
    dwr_ref,
    sk_ref,
    es_ref,
    s_buf,
    s_in,
    t_buf,
    t_in,
    zb_buf,
    zb_in,
    yb_buf,
    yb_in,
    g_buf,
    g_in,
    u_buf,
    u_in,
    vb_buf,
    vb_in,
    wb_buf,
    wb_in,
    tp_buf,
    tp_in,
    ny_buf,
    ny_in,
    nz_buf,
    nz_in,
    ly_buf,
    ly_in,
    lz_buf,
    lz_in,
    ssem,
    rsem,
):
    toks, cols_all = x_ref.shape
    heads = raw_ref.shape[0]
    pairs = heads // 2
    half = toks // 2
    inner = cols_all * ntp
    ctx = lax.axis_index("ctx")
    tp = lax.axis_index("tp")
    y = lax.rem(ctx, ny)
    z = lax.div(ctx, ny)

    def along_y(to):
        return {"ctx": z * ny + to}

    def along_z(to):
        return {"ctx": to * ny + y}

    def along_t(to):
        return {"tp": to}

    lines = {"y": (ny, y, along_y), "z": (nz, z, along_z), "t": (ntp, tp, along_t)}

    barrier = pltpu.get_barrier_semaphore()
    partners = 0
    for count, me, where in lines.values():
        for d in range(1, count):
            pl.semaphore_signal(
                barrier,
                inc=1,
                device_id=where(lax.rem(me + d, count)),
                device_id_type=MESH,
            )
            partners += 1
    pl.semaphore_wait(barrier, partners)

    def exchange(slot, line, src, dst, spread):
        count, me, where = lines[line]
        made = []
        for d in range(1, count):
            to = lax.rem(me + d, count)
            made.append(
                pltpu.make_async_remote_copy(
                    src_ref=src.at[to] if spread else src,
                    dst_ref=dst.at[d],
                    send_sem=ssem.at[slot, d],
                    recv_sem=rsem.at[slot, d],
                    device_id=where(to),
                    device_id_type=MESH,
                )
            )
        for c in made:
            c.start()
        return made

    def arrived(made):
        for c in made:
            c.wait_recv()

    def sent(made):
        for c in made:
            c.wait_send()

    def from_y(k):
        return lax.rem(y + ny - k, ny)

    def from_z(k):
        return lax.rem(z + nz - k, nz)

    def cols_of(j):
        return pl.ds(pl.multiple_of(j * N, N), N)

    lane_low = iota((1, N), 1) < P_SIZE

    def lane_head(j):
        return 2 * j + jnp.where(lane_low, 0, 1)

    eye = iota((heads, heads), 0) == iota((heads, heads), 1)

    def column(row):
        return jnp.sum(
            jnp.where(eye, jnp.broadcast_to(row, (heads, heads)), 0.0), axis=1, keepdims=True
        )

    def row_of(col):
        return jnp.sum(
            jnp.where(eye, jnp.broadcast_to(col, (heads, heads)), 0.0), axis=0, keepdims=True
        )

    bias_raw = raw_ref[...] + column(bias_ref[...])
    delta = jnp.maximum(bias_raw, 0.0) + jnp.log1p(jnp.exp(-jnp.abs(bias_raw)))
    rate = jnp.exp(column(decay_ref[...]))
    skip_col = column(skip_ref[...])
    upto = (iota((toks, toks), 0) <= iota((toks, toks), 1)).astype(F32).astype(BF)
    a = nn3(-rate * delta, upto)
    a_end = a[:, toks - 1 : toks]
    dl_row[...] = delta
    stack = [a, jnp.exp(a), jnp.exp(a_end - a) * delta, delta]
    if 4 * heads < N:
        stack.append(jnp.zeros((N - 4 * heads, toks), F32))
    hi, mid, _ = split3(jnp.transpose(jnp.concatenate(stack, axis=0)))
    st_hi[...] = hi
    st_mid[...] = mid
    parts = [p.astype(F32) for p in split3(a)]
    for i in range(3):
        ahl_ref[i] = parts[i]
    tall = parts + [jnp.ones((8, toks), F32), jnp.zeros((N - 3 * heads - 8, toks), F32)]
    lhs_ref[...] = jnp.transpose(jnp.concatenate(tall, axis=0)).astype(BF)

    end_rows = jnp.broadcast_to(a_end, (heads, N))
    for h in range(heads):
        s_buf[h % ny, nz * P_SIZE + h // ny : nz * P_SIZE + h // ny + 1, :] = end_rows[h : h + 1, :]
    if nz < 8:
        for k in range(ny):
            s_buf[k, nz * P_SIZE + nz :, :] = jnp.zeros((8 - nz, N), F32)

    def put_heads(buf, j, both):
        for i in range(2):
            h = 2 * j + i
            rows = pl.ds(pl.multiple_of(lax.div(h, ny) * P_SIZE, P_SIZE), P_SIZE)
            buf[lax.rem(h, ny), rows, :] = both[i * P_SIZE : (i + 1) * P_SIZE, :]

    def take_heads(buf, j):
        got = []
        for i in range(2):
            h = 2 * j + i
            rows = pl.ds(pl.multiple_of(lax.div(h, ny) * P_SIZE, P_SIZE), P_SIZE)
            got.append(buf[from_y(lax.rem(h, ny)), rows, :])
        return jnp.concatenate(got, axis=0)

    def take_own(buf, j):
        got = []
        for i in range(2):
            h = 2 * j + i
            rows = pl.ds(pl.multiple_of(lax.div(h, ny) * P_SIZE, P_SIZE), P_SIZE)
            got.append(buf[lax.rem(h, ny), rows, :])
        return jnp.concatenate(got, axis=0)

    def first(j, _):
        cols = cols_of(j)
        place = jnp.concatenate(
            [(iota((N, N), 0) == q * heads + lane_head(j)).astype(F32) for q in (1, 2, 3)], axis=1
        ).astype(BF)
        wide = nn(st_hi[...], place) + nn(st_mid[...], place)
        e_ref[:, cols] = wide[:, :N]
        te_ref[:, cols] = wide[:, N : 2 * N]
        dl_ref[:, cols] = wide[:, 2 * N :]
        scaled = (x_ref[:, cols].astype(F32) * wide[:, N : 2 * N]).astype(BF)
        xs_ref[:, cols] = scaled
        put_heads(s_buf, j, tn(scaled, w_ref[...]))
        return 0

    lax.fori_loop(0, pairs, first, 0)
    y_there = exchange(0, "y", s_buf, s_in, True)
    s_in[0] = s_buf[y]

    causal = iota((toks, toks), 0) >= iota((toks, toks), 1)
    rwm_ref[...] = jnp.where(causal, nt(r_ref[...], w_ref[...]), 0.0)
    rwt_ref[...] = jnp.where(
        iota((toks, toks), 0) <= iota((toks, toks), 1), nt(w_ref[...], r_ref[...]), 0.0
    )

    def intra(j, _):
        cols = cols_of(j)
        xp = x_ref[:, cols]
        made = []
        row = iota((N, toks), 0)
        for i in range(2):
            h = 2 * j + i
            rhs = jnp.where((row == h) | (row == heads + h) | (row == 2 * heads + h), 1.0, 0.0)
            for k in range(3):
                rhs = jnp.where(row == 3 * heads + k, -ahl_ref[k, pl.ds(h, 1), :], rhs)
            rhs = rhs.astype(BF)
            rhs_ref[h] = rhs
            d_row = dl_row[pl.ds(h, 1), :]
            gap = nn(lhs_ref[:half, :], rhs[:, :half])
            m = (rwm_ref[:half, :half] * jnp.exp(jnp.minimum(gap, 0.0)) * d_row[:, :half]).astype(BF)
            top = nn(m, xp[:half])
            gap = nn(lhs_ref[half:, :], rhs)
            m = (rwm_ref[half:, :] * jnp.exp(jnp.minimum(gap, 0.0)) * d_row).astype(BF)
            made.append(jnp.concatenate([top, nn(m, xp)], axis=0))
        yi = jnp.where(lane_low, made[0], made[1])
        skip_row = jnp.sum(
            jnp.where(iota((heads, N), 0) == lane_head(j), skip_col, 0.0), axis=0, keepdims=True
        )
        ssd_ref[:, cols] = yi + skip_row * xp.astype(F32)
        gate = g_ref[:, cols].astype(F32)
        sig_ref[:, cols] = 1.0 / (1.0 + jnp.exp(-gate))
        return 0

    lax.fori_loop(0, pairs, intra, 0)
    arrived(y_there)

    def rows_z(k):
        return slice(k * P_SIZE, (k + 1) * P_SIZE)

    def log_end(k, j):
        return s_in[from_y(k), nz * P_SIZE + j : nz * P_SIZE + j + 1, :]

    for j in range(nz):
        total = s_in[from_y(0), rows_z(j), :]
        log_sum = log_end(0, j)
        for k in range(1, ny):
            total = jnp.exp(log_end(k, j)) * total + s_in[from_y(k), rows_z(j), :]
            log_sum = log_sum + log_end(k, j)
        t_buf[j, :P_SIZE, :] = total
        t_buf[j, P_SIZE:, :] = jnp.broadcast_to(log_sum, (8, N))
    z_there = exchange(1, "z", t_buf, t_in, True)
    t_in[0] = t_buf[z]
    arrived(z_there)

    state = start_ref[...]
    for k in range(nz):
        zb_buf[k] = state
        here = from_z(k)
        state = jnp.exp(t_in[here, P_SIZE : P_SIZE + 1, :]) * state + t_in[here, :P_SIZE, :]
    fin_ref[...] = state
    z_back = exchange(2, "z", zb_buf, zb_in, True)
    zb_in[0] = zb_buf[z]
    arrived(z_back)

    for j in range(nz):
        state = zb_in[from_z(j)]
        for k in range(ny):
            yb_buf[k, rows_z(j), :] = state
            if k < ny - 1:
                state = jnp.exp(log_end(k, j)) * state + s_in[from_y(k), rows_z(j), :]
    y_back = exchange(3, "y", yb_buf, yb_in, True)
    yb_in[0] = yb_buf[y]
    arrived(y_back)

    acc_ref[...] = jnp.zeros_like(acc_ref)

    def read(j, _):
        cols = cols_of(j)
        inc = take_heads(yb_in, j).astype(BF)
        ssd = ssd_ref[:, cols] + e_ref[:, cols] * nt(r_ref[...], inc)
        ssd_ref[:, cols] = ssd
        v = ssd * (g_ref[:, cols].astype(F32) * sig_ref[:, cols])
        v_ref[:, cols] = v
        acc_ref[0] += v * v
        acc_ref[1] += v * (og_ref[:, cols].astype(F32) * gain_ref[:, cols])
        return 0

    lax.fori_loop(0, pairs, read, 0)
    tp_buf[0:1, :] = jnp.sum(jnp.transpose(acc_ref[0]), axis=0, keepdims=True)
    tp_buf[1:2, :] = jnp.sum(jnp.transpose(acc_ref[1]), axis=0, keepdims=True)
    tp_buf[2:, :] = jnp.zeros((6, toks), F32)
    tp_sums = exchange(4, "t", tp_buf, tp_in, False)
    tp_in[0] = tp_buf[...]
    arrived(tp_sums)
    both = tp_in[0]
    for k in range(1, ntp):
        both = both + tp_in[k]
    inverse = lax.rsqrt(both[0:1, :] / inner + EPS)
    slope = inverse * inverse * inverse * both[1:2, :] / inner
    invk_ref[0] = jnp.transpose(jnp.broadcast_to(inverse, (N, toks)))
    invk_ref[1] = jnp.transpose(jnp.broadcast_to(slope, (N, toks)))

    def back(j, _):
        cols = cols_of(j)
        sg = og_ref[:, cols].astype(F32) * gain_ref[:, cols]
        dv = invk_ref[0] * sg - v_ref[:, cols] * invk_ref[1]
        d = dv * (g_ref[:, cols].astype(F32) * sig_ref[:, cols])
        d_ref[:, cols] = d.astype(BF)
        de = (d * e_ref[:, cols]).astype(BF)
        de_ref[:, cols] = de
        put_heads(g_buf, j, tn(de, r_ref[...]))
        return 0

    lax.fori_loop(0, pairs, back, 0)
    g_there = exchange(5, "y", g_buf, g_in, True)
    g_in[0] = g_buf[y]

    rk_ref[...] = jnp.zeros_like(rk_ref)
    dwr_ref[...] = jnp.zeros_like(dwr_ref)
    drwt_ref[...] = jnp.zeros_like(drwt_ref)

    def skip_of(j):
        return jnp.sum(
            jnp.where(iota((heads, N), 0) == lane_head(j), skip_col, 0.0), axis=0, keepdims=True
        )

    def gather_heads(j, prod):
        place = (
            iota((N, N), 1) == 2 * j + jnp.where(iota((N, N), 0) < P_SIZE, 0, 1)
        ).astype(F32).astype(BF)
        hi = prod.astype(BF)
        lo = (prod - hi.astype(F32)).astype(BF)
        return nn(hi, place) + nn(lo, place)

    def outs(j, _):
        cols = cols_of(j)
        og = og_ref[:, cols].astype(F32)
        gain = gain_ref[:, cols]
        v = v_ref[:, cols]
        ssd = ssd_ref[:, cols]
        vi = v * invk_ref[0]
        out_ref[:, cols] = (vi * gain).astype(BF)
        ny_buf[pl.ds(j, 1), :] = jnp.sum(og * vi, axis=0, keepdims=True)
        dv = invk_ref[0] * (og * gain) - v * invk_ref[1]
        gate = g_ref[:, cols].astype(F32)
        sig = sig_ref[:, cols]
        dg_ref[:, cols] = (dv * ssd * sig * (1.0 + gate * (1.0 - sig))).astype(BF)
        x = x_ref[:, cols].astype(F32)
        d = d_ref[:, cols].astype(F32)
        sk = jnp.sum(dv * (gate * sig) * x, axis=0, keepdims=True)
        sk_ref[pl.ds(2 * j, 1), :] = jnp.where(lane_low, sk, 0.0)
        sk_ref[pl.ds(2 * j + 1, 1), :] = jnp.where(lane_low, 0.0, sk)
        rk_ref[0] += gather_heads(j, d * (ssd - skip_of(j) * x))
        dwr_ref[1] += nn(de_ref[:, cols], take_heads(yb_in, j).astype(BF))
        return 0

    lax.fori_loop(0, pairs, outs, 0)

    def intra_back(j, _):
        cols = cols_of(j)
        dl = dl_ref[:, cols]
        xd = (x_ref[:, cols].astype(F32) * dl).astype(BF)
        dp = d_ref[:, cols]
        made = []
        sums = None
        for i in range(2):
            h = 2 * j + i
            keep = lane_low if i == 0 else jnp.logical_not(lane_low)
            mine = jnp.where(keep, dp.astype(F32), 0.0).astype(BF)
            rhs = rhs_ref[h]
            decay = jnp.exp(jnp.minimum(-nn(lhs_ref[:half, :], rhs), 0.0))
            upper = nt(xd[:half], mine) * decay
            top = nn((rwt_ref[:half, :] * decay).astype(BF), dp)
            decay = jnp.exp(jnp.minimum(-nn(lhs_ref[half:, :], rhs[:, half:]), 0.0))
            lower = nt(xd[half:], mine[half:]) * decay
            low = nn((rwt_ref[half:, half:] * decay).astype(BF), dp[half:])
            made.append(jnp.concatenate([top, low], axis=0))
            sums = (upper, lower) if sums is None else (sums[0] + upper, sums[1] + lower)
        drwt_ref[:half, :] += sums[0]
        drwt_ref[half:, half:] += sums[1]
        dxi_ref[:, cols] = jnp.where(lane_low, made[0], made[1]) * dl
        return 0

    lax.fori_loop(0, pairs, intra_back, 0)
    arrived(g_there)

    for j in range(nz):
        total = g_in[from_y(ny - 1), rows_z(j), :]
        for k in range(ny - 2, -1, -1):
            total = jnp.exp(log_end(k, j)) * total + g_in[from_y(k), rows_z(j), :]
        u_buf[j] = total
    u_there = exchange(6, "z", u_buf, u_in, True)
    u_in[0] = u_buf[z]
    arrived(u_there)
    state = jnp.zeros((P_SIZE, N), F32)
    for k in range(nz - 1, -1, -1):
        vb_buf[k] = state
        here = from_z(k)
        state = jnp.exp(t_in[here, P_SIZE : P_SIZE + 1, :]) * state + u_in[here]
    v_back = exchange(7, "z", vb_buf, vb_in, True)
    vb_in[0] = vb_buf[z]
    arrived(v_back)
    for j in range(nz):
        state = vb_in[from_z(j)]
        for k in range(ny - 1, -1, -1):
            wb_buf[k, rows_z(j), :] = state
            if k > 0:
                state = jnp.exp(log_end(k, j)) * state + g_in[from_y(k), rows_z(j), :]
    w_back = exchange(8, "y", wb_buf, wb_in, True)
    wb_in[0] = wb_buf[y]

    below = iota((toks, toks), 0) <= iota((toks, toks), 1)
    drwt = jnp.where(below, drwt_ref[...], 0.0).astype(BF)
    dr_in = tn(drwt, w_ref[...])
    dr_ref[...] = (dr_in.astype(BF).astype(F32) + dwr_ref[1].astype(BF).astype(F32)).astype(BF)
    dw_in = nn(drwt, r_ref[...])
    skip_sum = row_of(jnp.sum(sk_ref[...], axis=1, keepdims=True))
    ny_buf[pairs:, :] = jnp.zeros((ny_buf.shape[0] - pairs, N), F32)
    ny_buf[pairs : pairs + 1, :heads] = skip_sum
    sums_y = exchange(9, "y", ny_buf, ny_in, False)
    ny_in[0] = ny_buf[...]
    arrived(w_back)
    arrived(sums_y)
    total = ny_in[0]
    for k in range(1, ny):
        total = total + ny_in[k]
    nz_buf[...] = total
    sums_z = exchange(10, "z", nz_buf, nz_in, False)
    nz_in[0] = nz_buf[...]

    def last(j, _):
        cols = cols_of(j)
        later = take_heads(wb_in, j)
        inc = take_heads(yb_in, j)
        own = take_own(s_buf, j)
        for i in range(2):
            h = 2 * j + i
            end = s_buf[lax.rem(h, ny), pl.ds(nz * P_SIZE + lax.div(h, ny), 1), :]
            part = slice(i * P_SIZE, (i + 1) * P_SIZE)
            es_ref[pl.ds(h, 1), :] = jnp.sum(
                later[part] * (jnp.exp(end) * inc[part] + own[part]), axis=0, keepdims=True
            )
        later = later.astype(BF)
        state_part = nt(w_ref[...], later) * te_ref[:, cols]
        intra_part = dxi_ref[:, cols]
        x = x_ref[:, cols].astype(F32)
        rk_ref[1] += gather_heads(j, x * (intra_part + state_part))
        direct = (d_ref[:, cols].astype(F32) * skip_of(j)).astype(BF).astype(F32)
        joined = (intra_part.astype(BF).astype(F32) + state_part.astype(BF).astype(F32)).astype(BF)
        dx_ref[:, cols] = (joined.astype(F32) + direct).astype(BF)
        dwr_ref[0] += nn(xs_ref[:, cols], later)
        return 0

    lax.fori_loop(0, pairs, last, 0)
    dw_ref[...] = (dw_in.astype(BF).astype(F32) + dwr_ref[0].astype(BF).astype(F32)).astype(BF)

    k_rows = jnp.transpose(rk_ref[1])[:heads]
    d_log = jnp.transpose(rk_ref[0])[:heads] - k_rows
    end_sum = jnp.sum(es_ref[...], axis=1, keepdims=True)
    d_log = d_log + jnp.where(iota((heads, toks), 1) == toks - 1, end_sum, 0.0)
    from_on = (iota((toks, toks), 0) >= iota((toks, toks), 1)).astype(F32).astype(BF)
    d_inc = nn3(d_log, from_on)
    d_delta = k_rows / dl_row[...] - rate * d_inc
    again = raw_ref[...] + column(bias_ref[...])
    d_raw = d_delta * (1.0 / (1.0 + jnp.exp(-again)))
    dstep_ref[...] = d_raw
    ly_buf[...] = jnp.zeros_like(ly_buf)
    ly_buf[0:1, :heads] = row_of(jnp.sum(d_raw, axis=1, keepdims=True))
    ly_buf[1:2, :heads] = row_of(jnp.sum(d_inc * (-rate * dl_row[...]), axis=1, keepdims=True))
    late_y = exchange(11, "y", ly_buf, ly_in, False)
    ly_in[0] = ly_buf[...]
    arrived(late_y)
    total = ly_in[0]
    for k in range(1, ny):
        total = total + ly_in[k]
    lz_buf[...] = total
    late_z = exchange(12, "z", lz_buf, lz_in, False)
    lz_in[0] = lz_buf[...]
    arrived(sums_z)
    arrived(late_z)
    scale = 1.0 / math.sqrt(toks * ny * nz)
    total = nz_in[0]
    late = lz_in[0]
    for k in range(1, nz):
        total = total + nz_in[k]
        late = late + lz_in[k]
    for j in range(pairs):
        dnorm_ref[0:1, j * N : (j + 1) * N] = total[j : j + 1, :] * scale
    dheads_ref[0:2, :] = late[0:2, :heads] * scale
    dheads_ref[2:3, :] = total[pairs : pairs + 1, :heads] * scale
    for made in (
        y_there,
        z_there,
        z_back,
        y_back,
        tp_sums,
        g_there,
        u_there,
        v_back,
        w_back,
        sums_y,
        sums_z,
        late_y,
        late_z,
    ):
        sent(made)


def solution(mesh):
    nctx, ntp = mesh.shape["ctx"], mesh.shape["tp"]
    ny, nz = NY, nctx // NY

    def on_device(
        inputs,
        gate_input,
        write_proj,
        read_proj,
        step_raw,
        step_bias,
        decay_log,
        skip_gain,
        norm_gain,
        start_state,
        out_grad,
    ):
        toks, cols = inputs.shape
        heads = step_raw.shape[0]
        pairs = heads // 2
        group = nz * P_SIZE
        f32, bf = F32, BF

        def v(shape, dtype=f32):
            return pltpu.VMEM(shape, dtype)

        scratch = [
            v((toks, N), bf),
            v((toks, N), bf),
            v((toks, N), bf),
            v((heads, N, toks), bf),
            v((3, heads, toks)),
            v((heads, toks)),
            v((toks, cols)),
            v((toks, cols)),
            v((toks, cols)),
            v((toks, cols), bf),
            v((toks, cols)),
            v((toks, cols)),
            v((toks, cols)),
            v((toks, cols), bf),
            v((toks, cols), bf),
            v((toks, cols)),
            v((toks, toks)),
            v((toks, toks)),
            v((toks, toks)),
            v((2, toks, N)),
            v((2, toks, N)),
            v((2, toks, N)),
            v((2, toks, N)),
            v((heads, N)),
            v((heads, N)),
            v((ny, group + 8, N)),
            v((ny, group + 8, N)),
            v((nz, P_SIZE + 8, N)),
            v((nz, P_SIZE + 8, N)),
            v((nz, P_SIZE, N)),
            v((nz, P_SIZE, N)),
            v((ny, group, N)),
            v((ny, group, N)),
            v((ny, group, N)),
            v((ny, group, N)),
            v((nz, P_SIZE, N)),
            v((nz, P_SIZE, N)),
            v((nz, P_SIZE, N)),
            v((nz, P_SIZE, N)),
            v((ny, group, N)),
            v((ny, group, N)),
            v((8, toks)),
            v((ntp, 8, toks)),
            v((pairs + 8, N)),
            v((ny, pairs + 8, N)),
            v((pairs + 8, N)),
            v((nz, pairs + 8, N)),
            v((8, N)),
            v((ny, 8, N)),
            v((8, N)),
            v((nz, 8, N)),
            pltpu.SemaphoreType.DMA((13, 8)),
            pltpu.SemaphoreType.DMA((13, 8)),
        ]
        vmem = pl.BlockSpec(memory_space=pltpu.VMEM)
        shapes = [
            jax.ShapeDtypeStruct((toks, cols), bf),
            jax.ShapeDtypeStruct((P_SIZE, N), f32),
            jax.ShapeDtypeStruct((toks, cols), bf),
            jax.ShapeDtypeStruct((toks, cols), bf),
            jax.ShapeDtypeStruct((toks, N), bf),
            jax.ShapeDtypeStruct((toks, N), bf),
            jax.ShapeDtypeStruct((heads, toks), f32),
            jax.ShapeDtypeStruct((3, heads), f32),
            jax.ShapeDtypeStruct((1, cols), f32),
        ]
        made = pl.pallas_call(
            functools.partial(kernel, ny, nz, ntp),
            out_shape=shapes,
            in_specs=[vmem] * 11,
            out_specs=[vmem] * 9,
            scratch_shapes=scratch,
            compiler_params=pltpu.CompilerParams(
                collective_id=0, has_side_effects=True, vmem_limit_bytes=60 * 2**20
            ),
        )(
            inputs,
            gate_input,
            write_proj,
            read_proj,
            step_raw,
            step_bias.reshape(1, heads),
            decay_log.reshape(1, heads),
            skip_gain.reshape(1, heads),
            norm_gain.reshape(1, cols),
            start_state.reshape(P_SIZE, N),
            out_grad,
        )
        output, final, dx, dg, dw, dr, dstep, dheads, dnorm = made
        return (
            output,
            final.reshape(1, 1, P_SIZE * N),
            dx,
            dg,
            dw,
            dr,
            dstep,
            dheads,
            dnorm.reshape(cols),
        )

    in_specs = (
        P("ctx", "tp"),
        P("ctx", "tp"),
        P("ctx", "tp"),
        P("ctx", "tp"),
        P("tp", "ctx"),
        P("tp"),
        P("tp"),
        P("tp"),
        P("tp"),
        P("tp", "ctx", None),
        P("ctx", "tp"),
    )
    out_specs = (
        P("ctx", "tp"),
        P("tp", "ctx", None),
        P("ctx", "tp"),
        P("ctx", "tp"),
        P("ctx", "tp"),
        P("ctx", "tp"),
        P("tp", "ctx"),
        P(None, "tp"),
        P("tp"),
    )
    return jax.shard_map(
        on_device, mesh=mesh, in_specs=in_specs, out_specs=out_specs, check_vma=False
    )
```

time: 876 us -> 147 us (0.17); the launches traced: 867 us -> 147 us
  waiting for transfers between devices: 574 us -> 0 us
  blocking collectives: 141 us -> 0 us
  Pallas kernels: 0 us -> 137 us
  other arithmetic: 74 us -> 0 us
  matrix products: 27.1 us -> 0 us
  local copies, waits for them, and re-layouts: 34.7 us -> 9.06 us
  between operations: 14.5 us -> 0.68 us
    all_gather x3 -> x0, waiting for transfers between devices: 493 us -> none  [the longest x2 422 us: carried_in(): gathered = jax.tree.map(lambda a: lax.all_gather(a, axis), part)]
    pallas_call x0 -> x1, Pallas kernels: none -> 137 us  [on_device(): pl.pallas_call(functools.partial(kernel, ny, nz, ntp), out_shape=shapes,...]
    psum x3 -> x0, blocking collectives: 101 us -> none  [the longest x1 75.7 us: on_device(): totals = lax.psum((norm_part, bias_part, decay_part, skip_part), 'ctx')]
    psum x1 -> x0, waiting for transfers between devices: 80.6 us -> none  [spread(): return lax.psum(jnp.where(mine, value, jnp.zeros_like(value)), axis)]
    add x37 -> x0, other arithmetic: 49.1 us -> none  [the longest x31 45.4 us: compose(): jnp.exp(second_part[0])[..., None] * first_part[1] + second_part[1]]
    all_gather x1 -> x0, blocking collectives: 40.3 us -> none  [carried_in(): gathered = jax.tree.map(lambda a: lax.all_gather(a, axis), part)]
    dot_general x12 -> x0, matrix products: 27.1 us -> none  [the longest x3 15.6 us: local_parts(): jnp.einsum('ghkij,kjghp->kighp', mixing, input_blocks, preferred_element_...]
    exp x31 -> x0, local copies, waits for them, and re-layouts: 17.4 us -> none  [compose(): jnp.exp(second_part[0])[..., None] * first_part[1] + second_part[1]]
  transfers between devices with their start and end apart: 4 -> 0, of which waited for: 4 -> 0; matrix products, arithmetic and copies ran while one was open for 6% -> 0% of each run, Pallas kernels for 0% -> 0%
where the time goes in v1:
time: 147 us
  Pallas kernels  137 us (93%)
  local copies, waits for them, and re-layouts  9.06 us (6%)
    pallas_call x1, Pallas kernels, on_device(): pl.pallas_call(functools.partial(kernel, ny, nz, ntp), out_shape=shapes,...  137 us
    unnamed x25, local copies, waits for them, and re-layouts  9.06 us

profile of v1, /device:TPU:32, one launch (start us, length us, event | category | flops | bytes accessed | tf_op | source)
XLA Modules:
  0.0 147.0 jit_solution(7144113431348938540)
XLA Ops:
  0.6 137.2 %shard_map.178 = (bf16[256,2048]{1,0:T(8,128)(2,1)}, f32[64,128]{1,0:T(8,128)}, bf16[256,2048]{1,0:T(8,128)(2,1)}, bf16[256,2048]{1,0:T(8,128)(2,1)}, bf16[256,1...) custom-call(bf16[256,2048]{1,0:T(8,128)(2,1)} %x_ref.1, ...), custom_call_target="tpu_custom_call" | custom-call | tf_op jit(solution)/shard_map/pallas_call | solution.py:686
  137.9 0.0 copy-start.5
  137.9 0.0 copy-start.1
  137.9 2.4 %copy.29 = bf16[256,2048]{1,0:T(8,128)(2,1)} copy(bf16[256,2048]{1,0:T(8,128)(2,1)} %get-tuple-element.36) | data formatting | bytes 2097152
  140.3 0.0 copy-done.5
  140.3 0.6 copy.30
  140.9 0.0 copy-done.1
  140.9 0.0 copy-start
  140.9 1.0 copy.31
  141.9 0.6 copy-done
  142.5 0.0 copy-start.3
  142.5 1.0 copy.32
  143.5 0.0 copy-done.3
  143.5 0.0 copy-start.2
  143.5 0.6 copy.33
  144.1 0.2 copy-done.2
  144.4 0.0 copy-start.4
  144.4 0.0 copy-start.6
  144.4 0.6 copy.34
  145.0 0.1 copy-done.4
  145.1 0.0 copy-start.7
  145.1 0.6 copy.35
  145.7 0.1 copy-done.7
  145.8 0.6 copy.36
  146.4 0.0 copy-done.6
  146.4 0.6 copy.37
Async XLA Ops:
  137.9 2.4 %copy-start.5 = (f32[64,128]{1,0:T(8,128)S(1)}, f32[64,128]{1,0:T(8,128)}, u32[]{:S(2)}) copy-start(f32[64,128]{1,0:T(8,128)} %get-tuple-element.19) | copy-start | bytes 98308
  137.9 3.0 %copy-start.1 = (bf16[256,2048]{1,0:T(8,128)(2,1)S(1)}, bf16[256,2048]{1,0:T(8,128)(2,1)}, u32[]{:S(2)}) copy-start(bf16[256,2048]{1,0:T(8,128)(2,1)} %get-tuple-element.38) | copy-start | bytes 3145732
  140.9 1.6 %copy-start = (bf16[256,2048]{1,0:T(8,128)(2,1)S(1)}, bf16[256,2048]{1,0:T(8,128)(2,1)}, u32[]{:S(2)}) copy-start(bf16[256,2048]{1,0:T(8,128)(2,1)} %get-tuple-element.39) | copy-start | bytes 3145732
  142.5 1.0 copy-start.3
  143.5 0.9 copy-start.2
  144.4 0.8 copy-start.4
  144.4 2.0 %copy-start.6 = (f32[1,2048]{1,0:T(1,128)S(1)}, f32[1,2048]{1,0:T(1,128)}, u32[]{:S(2)}) copy-start(f32[1,2048]{1,0:T(1,128)} %get-tuple-element.26) | copy-start | bytes 24580
  145.1 0.7 copy-start.7

commit v2 on v1

--- a/solution.py
+++ b/solution.py
@@ -12,6 +12,9 @@
 N = 128
 NY = 4
 EPS = 1e-05
+SLOTS = 11 + 4 * 4
+CHUNKS = 4
+UNROLL = 4
 F32 = jnp.float32
 BF = jnp.bfloat16
 MESH = pl.DeviceIdType.MESH
@@ -83,6 +86,7 @@
     e_ref,
     dl_ref,
     xs_ref,
+    xd_ref,
     ssd_ref,
     sig_ref,
     v_ref,
@@ -98,6 +102,13 @@
     dwr_ref,
     sk_ref,
     es_ref,
+    lg_buf,
+    lg_in,
+    lr_buf,
+    lr_in,
+    f_own,
+    f_ref,
+    fz_ref,
     s_buf,
     s_in,
     t_buf,
@@ -161,15 +172,18 @@
             partners += 1
     pl.semaphore_wait(barrier, partners)
 
-    def exchange(slot, line, src, dst, spread):
+    slots = iter(range(SLOTS))
+
+    def exchange(line, src, dst):
+        slot = next(slots)
         count, me, where = lines[line]
         made = []
         for d in range(1, count):
             to = lax.rem(me + d, count)
             made.append(
                 pltpu.make_async_remote_copy(
-                    src_ref=src.at[to] if spread else src,
-                    dst_ref=dst.at[d],
+                    src_ref=src(to),
+                    dst_ref=dst(d),
                     send_sem=ssem.at[slot, d],
                     recv_sem=rsem.at[slot, d],
                     device_id=where(to),
@@ -178,15 +192,23 @@
             )
         for c in made:
             c.start()
+        started.append(lambda: [c.wait_send() for c in made])
         return made
+
+    started = []
 
     def arrived(made):
         for c in made:
             c.wait_recv()
 
-    def sent(made):
-        for c in made:
-            c.wait_send()
+    def whole(ref):
+        return lambda to: ref
+
+    def at(ref):
+        return lambda d: ref.at[d]
+
+    def at_rows(ref, rows):
+        return lambda d: ref.at[d, rows]
 
     def from_y(k):
         return lax.rem(y + ny - k, ny)
@@ -235,11 +257,12 @@
     lhs_ref[...] = jnp.transpose(jnp.concatenate(tall, axis=0)).astype(BF)
 
     end_rows = jnp.broadcast_to(a_end, (heads, N))
+    lg_buf[...] = jnp.zeros_like(lg_buf)
     for h in range(heads):
-        s_buf[h % ny, nz * P_SIZE + h // ny : nz * P_SIZE + h // ny + 1, :] = end_rows[h : h + 1, :]
-    if nz < 8:
-        for k in range(ny):
-            s_buf[k, nz * P_SIZE + nz :, :] = jnp.zeros((8 - nz, N), F32)
+        lg_buf[h % ny, h // ny : h // ny + 1, :] = end_rows[h : h + 1, :]
+    f_own[...] = jnp.exp(lg_buf[...])
+    logs_y = exchange("y", at(lg_buf), at(lg_in))
+    lg_in[0] = lg_buf[y]
 
     def put_heads(buf, j, both):
         for i in range(2):
@@ -255,13 +278,14 @@
             got.append(buf[from_y(lax.rem(h, ny)), rows, :])
         return jnp.concatenate(got, axis=0)
 
-    def take_own(buf, j):
-        got = []
-        for i in range(2):
-            h = 2 * j + i
-            rows = pl.ds(pl.multiple_of(lax.div(h, ny) * P_SIZE, P_SIZE), P_SIZE)
-            got.append(buf[lax.rem(h, ny), rows, :])
-        return jnp.concatenate(got, axis=0)
+    per_chunk = nz // CHUNKS
+
+    def loop(body, c, unroll=UNROLL):
+        n = pairs // CHUNKS
+        lax.fori_loop(c * n, (c + 1) * n, body, 0, unroll=min(n, unroll))
+
+    def chunk_rows(c):
+        return slice(c * per_chunk * P_SIZE, (c + 1) * per_chunk * P_SIZE)
 
     def first(j, _):
         cols = cols_of(j)
@@ -272,24 +296,21 @@
         e_ref[:, cols] = wide[:, :N]
         te_ref[:, cols] = wide[:, N : 2 * N]
         dl_ref[:, cols] = wide[:, 2 * N :]
-        scaled = (x_ref[:, cols].astype(F32) * wide[:, N : 2 * N]).astype(BF)
+        x = x_ref[:, cols].astype(F32)
+        scaled = (x * wide[:, N : 2 * N]).astype(BF)
         xs_ref[:, cols] = scaled
+        xd_ref[:, cols] = (x * wide[:, 2 * N :]).astype(BF)
         put_heads(s_buf, j, tn(scaled, w_ref[...]))
         return 0
 
-    lax.fori_loop(0, pairs, first, 0)
-    y_there = exchange(0, "y", s_buf, s_in, True)
-    s_in[0] = s_buf[y]
-
-    causal = iota((toks, toks), 0) >= iota((toks, toks), 1)
-    rwm_ref[...] = jnp.where(causal, nt(r_ref[...], w_ref[...]), 0.0)
-    rwt_ref[...] = jnp.where(
-        iota((toks, toks), 0) <= iota((toks, toks), 1), nt(w_ref[...], r_ref[...]), 0.0
-    )
+    def skip_of(j):
+        return jnp.sum(
+            jnp.where(iota((heads, N), 0) == lane_head(j), skip_col, 0.0), axis=0, keepdims=True
+        )
 
     def intra(j, _):
         cols = cols_of(j)
-        xp = x_ref[:, cols]
+        xd = xd_ref[:, cols]
         made = []
         row = iota((N, toks), 0)
         for i in range(2):
@@ -299,64 +320,130 @@
                 rhs = jnp.where(row == 3 * heads + k, -ahl_ref[k, pl.ds(h, 1), :], rhs)
             rhs = rhs.astype(BF)
             rhs_ref[h] = rhs
-            d_row = dl_row[pl.ds(h, 1), :]
             gap = nn(lhs_ref[:half, :], rhs[:, :half])
-            m = (rwm_ref[:half, :half] * jnp.exp(jnp.minimum(gap, 0.0)) * d_row[:, :half]).astype(BF)
-            top = nn(m, xp[:half])
+            m = (rwm_ref[:half, :half] * jnp.exp(jnp.minimum(gap, 0.0))).astype(BF)
+            top = nn(m, xd[:half])
             gap = nn(lhs_ref[half:, :], rhs)
-            m = (rwm_ref[half:, :] * jnp.exp(jnp.minimum(gap, 0.0)) * d_row).astype(BF)
-            made.append(jnp.concatenate([top, nn(m, xp)], axis=0))
+            m = (rwm_ref[half:, :] * jnp.exp(jnp.minimum(gap, 0.0))).astype(BF)
+            made.append(jnp.concatenate([top, nn(m, xd)], axis=0))
         yi = jnp.where(lane_low, made[0], made[1])
-        skip_row = jnp.sum(
-            jnp.where(iota((heads, N), 0) == lane_head(j), skip_col, 0.0), axis=0, keepdims=True
-        )
-        ssd_ref[:, cols] = yi + skip_row * xp.astype(F32)
+        ssd_ref[:, cols] = yi + skip_of(j) * x_ref[:, cols].astype(F32)
         gate = g_ref[:, cols].astype(F32)
         sig_ref[:, cols] = 1.0 / (1.0 + jnp.exp(-gate))
         return 0
 
-    lax.fori_loop(0, pairs, intra, 0)
-    arrived(y_there)
-
     def rows_z(k):
         return slice(k * P_SIZE, (k + 1) * P_SIZE)
 
-    def log_end(k, j):
-        return s_in[from_y(k), nz * P_SIZE + j : nz * P_SIZE + j + 1, :]
-
-    for j in range(nz):
-        total = s_in[from_y(0), rows_z(j), :]
-        log_sum = log_end(0, j)
-        for k in range(1, ny):
-            total = jnp.exp(log_end(k, j)) * total + s_in[from_y(k), rows_z(j), :]
-            log_sum = log_sum + log_end(k, j)
-        t_buf[j, :P_SIZE, :] = total
-        t_buf[j, P_SIZE:, :] = jnp.broadcast_to(log_sum, (8, N))
-    z_there = exchange(1, "z", t_buf, t_in, True)
-    t_in[0] = t_buf[z]
-    arrived(z_there)
-
-    state = start_ref[...]
-    for k in range(nz):
-        zb_buf[k] = state
-        here = from_z(k)
-        state = jnp.exp(t_in[here, P_SIZE : P_SIZE + 1, :]) * state + t_in[here, :P_SIZE, :]
-    fin_ref[...] = state
-    z_back = exchange(2, "z", zb_buf, zb_in, True)
-    zb_in[0] = zb_buf[z]
-    arrived(z_back)
-
-    for j in range(nz):
-        state = zb_in[from_z(j)]
-        for k in range(ny):
-            yb_buf[k, rows_z(j), :] = state
-            if k < ny - 1:
-                state = jnp.exp(log_end(k, j)) * state + s_in[from_y(k), rows_z(j), :]
-    y_back = exchange(3, "y", yb_buf, yb_in, True)
-    yb_in[0] = yb_buf[y]
-    arrived(y_back)
-
-    acc_ref[...] = jnp.zeros_like(acc_ref)
+    def heads_of(c):
+        return range(c * per_chunk, (c + 1) * per_chunk)
+
+    def send_y(buf, into, c):
+        rows = chunk_rows(c)
+        made = exchange("y", at_rows(buf, rows), at_rows(into, rows))
+        into[0, rows, :] = buf[y, rows, :]
+        return made
+
+    def to_owner(slot, buf, into, t):
+        return pltpu.make_async_remote_copy(
+            src_ref=buf.at[t],
+            dst_ref=into.at[z],
+            send_sem=ssem.at[slot, t],
+            recv_sem=rsem.at[slot, z],
+            device_id=along_z(t),
+            device_id_type=MESH,
+        )
+
+    def from_sender(slot, buf, into, k):
+        return pltpu.make_async_remote_copy(
+            src_ref=buf.at[z],
+            dst_ref=into.at[k],
+            send_sem=ssem.at[slot, z],
+            recv_sem=rsem.at[slot, k],
+            device_id=along_z(k),
+            device_id_type=MESH,
+        )
+
+    def to_row(slot, buf, into, d):
+        to = lax.rem(z + d, nz)
+        return pltpu.make_async_remote_copy(
+            src_ref=buf.at[to],
+            dst_ref=into.at[z],
+            send_sem=ssem.at[slot, d],
+            recv_sem=rsem.at[slot, z],
+            device_id=along_z(to),
+            device_id_type=MESH,
+        )
+
+    class Scan:
+        def __init__(self, buf, into, back_buf, back_in):
+            self.there, self.back = next(slots), next(slots)
+            self.buf, self.into, self.back_buf, self.back_in = buf, into, back_buf, back_in
+
+        def send(self, c):
+            for t in heads_of(c):
+
+                @pl.when(z != t)
+                def _():
+                    to_owner(self.there, self.buf, self.into, t).start()
+
+                @pl.when(z == t)
+                def _():
+                    self.into[t] = self.buf[t]
+
+        def scan(self, c, body):
+            @pl.when(lax.div(z, per_chunk) == c)
+            def _():
+                for d in range(1, nz):
+                    from_sender(self.there, self.buf, self.into, lax.rem(z + d, nz)).wait_recv()
+                body()
+                for d in range(1, nz):
+                    to_row(self.back, self.back_buf, self.back_in, d).start()
+                self.back_in[z] = self.back_buf[z]
+
+        def wait(self, c):
+            for t in heads_of(c):
+
+                @pl.when(z != t)
+                def _():
+                    from_sender(self.back, self.back_buf, self.back_in, t).wait_recv()
+
+        def sent(self):
+            for t in range(nz):
+
+                @pl.when(z != t)
+                def _():
+                    to_owner(self.there, self.buf, self.into, t).wait_send()
+
+            for d in range(1, nz):
+                to_row(self.back, self.back_buf, self.back_in, d).wait_send()
+
+    forward = Scan(t_buf, t_in, zb_buf, zb_in)
+
+    def compose(c):
+        for j in heads_of(c):
+            total = s_in[from_y(0), rows_z(j), :]
+            for k in range(1, ny):
+                total = f_ref[k, j : j + 1, :] * total + s_in[from_y(k), rows_z(j), :]
+            t_buf[j] = total
+        forward.send(c)
+
+    def scan_forward():
+        state = start_ref[...]
+        for k in range(nz):
+            zb_buf[k] = state
+            state = fz_ref[k : k + 1, :] * state + t_in[k]
+        fin_ref[...] = state
+
+    def expand(c):
+        forward.wait(c)
+        for j in heads_of(c):
+            state = zb_in[j]
+            for k in range(ny):
+                yb_buf[k, rows_z(j), :] = state
+                if k < ny - 1:
+                    state = f_ref[k, j : j + 1, :] * state + s_in[from_y(k), rows_z(j), :]
+        return send_y(yb_buf, yb_in, c)
 
     def read(j, _):
         cols = cols_of(j)
@@ -369,11 +456,58 @@
         acc_ref[1] += v * (og_ref[:, cols].astype(F32) * gain_ref[:, cols])
         return 0
 
-    lax.fori_loop(0, pairs, read, 0)
+    y_there, y_back = [], []
+    for c in range(CHUNKS):
+        loop(first, c)
+        y_there.append(send_y(s_buf, s_in, c))
+        if c == 1:
+            arrived(logs_y)
+            log_sum = jnp.zeros((8, N), F32)
+            for k in range(ny):
+                log_end = lg_in[from_y(k)]
+                f_ref[k] = jnp.exp(log_end)
+                log_sum = log_sum + log_end
+            lr_buf[...] = log_sum
+            logs_z = exchange("z", whole(lr_buf), at(lr_in))
+            lr_in[0] = log_sum
+    causal = iota((toks, toks), 0) >= iota((toks, toks), 1)
+    rwm_ref[...] = jnp.where(causal, nt(r_ref[...], w_ref[...]), 0.0)
+    rwt_ref[...] = jnp.where(
+        iota((toks, toks), 0) <= iota((toks, toks), 1), nt(w_ref[...], r_ref[...]), 0.0
+    )
+    acc_ref[...] = jnp.zeros_like(acc_ref)
+    arrived(y_there[0])
+    compose(0)
+    loop(intra, 0)
+    arrived(y_there[1])
+    compose(1)
+    loop(intra, 1)
+    arrived(y_there[2])
+    compose(2)
+    arrived(logs_z)
+    for k in range(nz):
+        fz_ref[k : k + 1, :] = jnp.exp(lr_in[from_z(k), pl.ds(z, 1), :])
+    forward.scan(0, scan_forward)
+    loop(intra, 2)
+    arrived(y_there[3])
+    compose(3)
+    forward.scan(1, scan_forward)
+    loop(intra, 3)
+    forward.scan(2, scan_forward)
+    y_back.append(expand(0))
+    forward.scan(3, scan_forward)
+    for c in range(1, 3):
+        y_back.append(expand(c))
+    arrived(y_back[0])
+    loop(read, 0)
+    y_back.append(expand(3))
+    for c in range(1, CHUNKS):
+        arrived(y_back[c])
+        loop(read, c)
     tp_buf[0:1, :] = jnp.sum(jnp.transpose(acc_ref[0]), axis=0, keepdims=True)
     tp_buf[1:2, :] = jnp.sum(jnp.transpose(acc_ref[1]), axis=0, keepdims=True)
     tp_buf[2:, :] = jnp.zeros((6, toks), F32)
-    tp_sums = exchange(4, "t", tp_buf, tp_in, False)
+    tp_sums = exchange("t", whole(tp_buf), at(tp_in))
     tp_in[0] = tp_buf[...]
     arrived(tp_sums)
     both = tp_in[0]
@@ -395,18 +529,9 @@
         put_heads(g_buf, j, tn(de, r_ref[...]))
         return 0
 
-    lax.fori_loop(0, pairs, back, 0)
-    g_there = exchange(5, "y", g_buf, g_in, True)
-    g_in[0] = g_buf[y]
-
     rk_ref[...] = jnp.zeros_like(rk_ref)
     dwr_ref[...] = jnp.zeros_like(dwr_ref)
     drwt_ref[...] = jnp.zeros_like(drwt_ref)
-
-    def skip_of(j):
-        return jnp.sum(
-            jnp.where(iota((heads, N), 0) == lane_head(j), skip_col, 0.0), axis=0, keepdims=True
-        )
 
     def gather_heads(j, prod):
         place = (
@@ -438,12 +563,9 @@
         dwr_ref[1] += nn(de_ref[:, cols], take_heads(yb_in, j).astype(BF))
         return 0
 
-    lax.fori_loop(0, pairs, outs, 0)
-
     def intra_back(j, _):
         cols = cols_of(j)
-        dl = dl_ref[:, cols]
-        xd = (x_ref[:, cols].astype(F32) * dl).astype(BF)
+        xd = xd_ref[:, cols]
         dp = d_ref[:, cols]
         made = []
         sums = None
@@ -462,80 +584,111 @@
             sums = (upper, lower) if sums is None else (sums[0] + upper, sums[1] + lower)
         drwt_ref[:half, :] += sums[0]
         drwt_ref[half:, half:] += sums[1]
-        dxi_ref[:, cols] = jnp.where(lane_low, made[0], made[1]) * dl
+        unscaled = jnp.where(lane_low, made[0], made[1])
+        v_ref[:, cols] = xd.astype(F32) * unscaled
+        dxi_ref[:, cols] = unscaled * dl_ref[:, cols]
         return 0
 
-    lax.fori_loop(0, pairs, intra_back, 0)
-    arrived(g_there)
-
-    for j in range(nz):
-        total = g_in[from_y(ny - 1), rows_z(j), :]
-        for k in range(ny - 2, -1, -1):
-            total = jnp.exp(log_end(k, j)) * total + g_in[from_y(k), rows_z(j), :]
-        u_buf[j] = total
-    u_there = exchange(6, "z", u_buf, u_in, True)
-    u_in[0] = u_buf[z]
-    arrived(u_there)
-    state = jnp.zeros((P_SIZE, N), F32)
-    for k in range(nz - 1, -1, -1):
-        vb_buf[k] = state
-        here = from_z(k)
-        state = jnp.exp(t_in[here, P_SIZE : P_SIZE + 1, :]) * state + u_in[here]
-    v_back = exchange(7, "z", vb_buf, vb_in, True)
-    vb_in[0] = vb_buf[z]
-    arrived(v_back)
-    for j in range(nz):
-        state = vb_in[from_z(j)]
-        for k in range(ny - 1, -1, -1):
-            wb_buf[k, rows_z(j), :] = state
-            if k > 0:
-                state = jnp.exp(log_end(k, j)) * state + g_in[from_y(k), rows_z(j), :]
-    w_back = exchange(8, "y", wb_buf, wb_in, True)
-    wb_in[0] = wb_buf[y]
+    backward = Scan(u_buf, u_in, vb_buf, vb_in)
+
+    def compose_back(c):
+        for j in heads_of(c):
+            total = g_in[from_y(ny - 1), rows_z(j), :]
+            for k in range(ny - 2, -1, -1):
+                total = f_ref[k, j : j + 1, :] * total + g_in[from_y(k), rows_z(j), :]
+            u_buf[j] = total
+        backward.send(c)
+
+    def scan_back():
+        state = jnp.zeros((P_SIZE, N), F32)
+        for k in range(nz - 1, -1, -1):
+            vb_buf[k] = state
+            state = fz_ref[k : k + 1, :] * state + u_in[k]
+
+    def expand_back(c):
+        backward.wait(c)
+        for j in heads_of(c):
+            state = vb_in[j]
+            for k in range(ny - 1, -1, -1):
+                wb_buf[k, rows_z(j), :] = state
+                if k > 0:
+                    state = f_ref[k, j : j + 1, :] * state + g_in[from_y(k), rows_z(j), :]
+        return send_y(wb_buf, wb_in, c)
+
+    g_there, w_back = [], []
+    for c in range(CHUNKS):
+        loop(back, c)
+        g_there.append(send_y(g_buf, g_in, c))
+    loop(outs, 0)
+    arrived(g_there[0])
+    compose_back(0)
+    loop(outs, 1)
+    arrived(g_there[1])
+    compose_back(1)
+    loop(outs, 2)
+    arrived(g_there[2])
+    compose_back(2)
+    loop(outs, 3)
+    skip_sum = row_of(jnp.sum(sk_ref[...], axis=1, keepdims=True))
+    ny_buf[pairs:, :] = jnp.zeros((ny_buf.shape[0] - pairs, N), F32)
+    ny_buf[pairs : pairs + 1, :heads] = skip_sum
+    sums_y = exchange("y", whole(ny_buf), at(ny_in))
+    ny_in[0] = ny_buf[...]
+    backward.scan(0, scan_back)
+    loop(intra_back, 0)
+    arrived(g_there[3])
+    compose_back(3)
+    backward.scan(1, scan_back)
+    loop(intra_back, 1)
+    backward.scan(2, scan_back)
+    w_back.append(expand_back(0))
+    loop(intra_back, 2)
+    backward.scan(3, scan_back)
+    for c in range(1, 3):
+        w_back.append(expand_back(c))
+    loop(intra_back, 3)
+    w_back.append(expand_back(3))
 
     below = iota((toks, toks), 0) <= iota((toks, toks), 1)
     drwt = jnp.where(below, drwt_ref[...], 0.0).astype(BF)
     dr_in = tn(drwt, w_ref[...])
     dr_ref[...] = (dr_in.astype(BF).astype(F32) + dwr_ref[1].astype(BF).astype(F32)).astype(BF)
     dw_in = nn(drwt, r_ref[...])
-    skip_sum = row_of(jnp.sum(sk_ref[...], axis=1, keepdims=True))
-    ny_buf[pairs:, :] = jnp.zeros((ny_buf.shape[0] - pairs, N), F32)
-    ny_buf[pairs : pairs + 1, :heads] = skip_sum
-    sums_y = exchange(9, "y", ny_buf, ny_in, False)
-    ny_in[0] = ny_buf[...]
-    arrived(w_back)
     arrived(sums_y)
     total = ny_in[0]
     for k in range(1, ny):
         total = total + ny_in[k]
     nz_buf[...] = total
-    sums_z = exchange(10, "z", nz_buf, nz_in, False)
+    sums_z = exchange("z", whole(nz_buf), at(nz_in))
     nz_in[0] = nz_buf[...]
 
     def last(j, _):
         cols = cols_of(j)
         later = take_heads(wb_in, j)
         inc = take_heads(yb_in, j)
-        own = take_own(s_buf, j)
-        for i in range(2):
-            h = 2 * j + i
-            end = s_buf[lax.rem(h, ny), pl.ds(nz * P_SIZE + lax.div(h, ny), 1), :]
-            part = slice(i * P_SIZE, (i + 1) * P_SIZE)
-            es_ref[pl.ds(h, 1), :] = jnp.sum(
-                later[part] * (jnp.exp(end) * inc[part] + own[part]), axis=0, keepdims=True
-            )
+        held = later * inc
         later = later.astype(BF)
         state_part = nt(w_ref[...], later) * te_ref[:, cols]
         intra_part = dxi_ref[:, cols]
         x = x_ref[:, cols].astype(F32)
-        rk_ref[1] += gather_heads(j, x * (intra_part + state_part))
+        written = x * state_part
+        rk_ref[1] += gather_heads(j, v_ref[:, cols] + written)
+        written = jnp.sum(written, axis=0, keepdims=True)
+        for i in range(2):
+            h = 2 * j + i
+            factor = f_own[lax.rem(h, ny), pl.ds(lax.div(h, ny), 1), :]
+            kept = jnp.sum(held[i * P_SIZE : (i + 1) * P_SIZE], axis=0, keepdims=True)
+            keep = lane_low if i == 0 else jnp.logical_not(lane_low)
+            es_ref[pl.ds(h, 1), :] = factor * kept + jnp.where(keep, written, 0.0)
         direct = (d_ref[:, cols].astype(F32) * skip_of(j)).astype(BF).astype(F32)
         joined = (intra_part.astype(BF).astype(F32) + state_part.astype(BF).astype(F32)).astype(BF)
         dx_ref[:, cols] = (joined.astype(F32) + direct).astype(BF)
         dwr_ref[0] += nn(xs_ref[:, cols], later)
         return 0
 
-    lax.fori_loop(0, pairs, last, 0)
+    for c in range(CHUNKS):
+        arrived(w_back[c])
+        loop(last, c)
     dw_ref[...] = (dw_in.astype(BF).astype(F32) + dwr_ref[0].astype(BF).astype(F32)).astype(BF)
 
     k_rows = jnp.transpose(rk_ref[1])[:heads]
@@ -551,14 +704,14 @@
     ly_buf[...] = jnp.zeros_like(ly_buf)
     ly_buf[0:1, :heads] = row_of(jnp.sum(d_raw, axis=1, keepdims=True))
     ly_buf[1:2, :heads] = row_of(jnp.sum(d_inc * (-rate * dl_row[...]), axis=1, keepdims=True))
-    late_y = exchange(11, "y", ly_buf, ly_in, False)
+    late_y = exchange("y", whole(ly_buf), at(ly_in))
     ly_in[0] = ly_buf[...]
     arrived(late_y)
     total = ly_in[0]
     for k in range(1, ny):
         total = total + ly_in[k]
     lz_buf[...] = total
-    late_z = exchange(12, "z", lz_buf, lz_in, False)
+    late_z = exchange("z", whole(lz_buf), at(lz_in))
     lz_in[0] = lz_buf[...]
     arrived(sums_z)
     arrived(late_z)
@@ -572,22 +725,20 @@
         dnorm_ref[0:1, j * N : (j + 1) * N] = total[j : j + 1, :] * scale
     dheads_ref[0:2, :] = late[0:2, :heads] * scale
     dheads_ref[2:3, :] = total[pairs : pairs + 1, :heads] * scale
-    for made in (
-        y_there,
-        z_there,
-        z_back,
-        y_back,
-        tp_sums,
-        g_there,
-        u_there,
-        v_back,
-        w_back,
-        sums_y,
-        sums_z,
-        late_y,
-        late_z,
-    ):
-        sent(made)
+    forward.sent()
+    backward.sent()
+    for wait in started:
+        wait()
+
+
+def copy_kernel(*refs):
+    n = (len(refs) - 1) // 2
+    sem = refs[-1]
+    made = [pltpu.make_async_copy(refs[i], refs[n + i], sem.at[i]) for i in range(n)]
+    for c in made:
+        c.start()
+    for c in made:
+        c.wait()
 
 
 def solution(mesh):
@@ -627,6 +778,7 @@
             v((toks, cols)),
             v((toks, cols)),
             v((toks, cols), bf),
+            v((toks, cols), bf),
             v((toks, cols)),
             v((toks, cols)),
             v((toks, cols)),
@@ -642,10 +794,17 @@
             v((2, toks, N)),
             v((heads, N)),
             v((heads, N)),
-            v((ny, group + 8, N)),
-            v((ny, group + 8, N)),
-            v((nz, P_SIZE + 8, N)),
-            v((nz, P_SIZE + 8, N)),
+            v((ny, 8, N)),
+            v((ny, 8, N)),
+            v((8, N)),
+            v((nz, 8, N)),
+            v((ny, 8, N)),
+            v((ny, 8, N)),
+            v((8, N)),
+            v((ny, group, N)),
+            v((ny, group, N)),
+            v((nz, P_SIZE, N)),
+            v((nz, P_SIZE, N)),
             v((nz, P_SIZE, N)),
             v((nz, P_SIZE, N)),
             v((ny, group, N)),
@@ -668,8 +827,8 @@
             v((ny, 8, N)),
             v((8, N)),
             v((nz, 8, N)),
-            pltpu.SemaphoreType.DMA((13, 8)),
-            pltpu.SemaphoreType.DMA((13, 8)),
+            pltpu.SemaphoreType.DMA((SLOTS, 8)),
+            pltpu.SemaphoreType.DMA((SLOTS, 8)),
         ]
         vmem = pl.BlockSpec(memory_space=pltpu.VMEM)
         shapes = [
@@ -705,6 +864,14 @@
             start_state.reshape(P_SIZE, N),
             out_grad,
         )
+        anywhere = pl.BlockSpec(memory_space=pl.ANY)
+        made = pl.pallas_call(
+            copy_kernel,
+            out_shape=shapes,
+            in_specs=[vmem] * 9,
+            out_specs=[anywhere] * 9,
+            scratch_shapes=[pltpu.SemaphoreType.DMA((9,))],
+        )(*made)
         output, final, dx, dg, dw, dr, dstep, dheads, dnorm = made
         return (
             output,

time: 147 us -> 107 us (0.73)
  Pallas kernels: 137 us -> 106 us
  local copies, waits for them, and re-layouts: 9.06 us -> 0 us
    pallas_call x1, Pallas kernels: 137 us -> 102 us  [on_device(): pl.pallas_call(functools.partial(kernel, ny, nz, ntp), out_shape=shapes,...]
    unnamed x25 -> x0, local copies, waits for them, and re-layouts: 9.06 us -> none
    pallas_call x0 -> x1, Pallas kernels: none -> 3.72 us  [on_device(): pl.pallas_call(copy_kernel, out_shape=shapes, in_specs=[vmem] * 9, out_sp...]
where the time goes in v2:
time: 107 us
  Pallas kernels  106 us (99%)
    pallas_call x1, Pallas kernels, on_device(): pl.pallas_call(functools.partial(kernel, ny, nz, ntp), out_shape=shapes,...  102 us
    pallas_call x1, Pallas kernels, on_device(): pl.pallas_call(copy_kernel, out_shape=shapes, in_specs=[vmem] * 9, out_sp...  3.72 us

profile of v2, /device:TPU:32, one launch (start us, length us, event | category | flops | bytes accessed | tf_op | source)
XLA Modules:
  0.0 106.6 jit_solution(14110436687716746266)
XLA Ops:
  0.6 102.1 %shard_map.178 = (bf16[256,2048]{1,0:T(8,128)(2,1)}, f32[64,128]{1,0:T(8,128)}, bf16[256,2048]{1,0:T(8,128)(2,1)}, bf16[256,2048]{1,0:T(8,128)(2,1)}, bf16[256,1...) custom-call(bf16[256,2048]{1,0:T(8,128)(2,1)} %x_ref.1, ...), custom_call_target="tpu_custom_call" | custom-call | tf_op jit(solution)/shard_map/pallas_call | solution.py:845
  102.7 3.7 %shard_map.179 = (bf16[256,2048]{1,0:T(8,128)(2,1)}, f32[64,128]{1,0:T(8,128)}, bf16[256,2048]{1,0:T(8,128)(2,1)}, bf16[256,2048]{1,0:T(8,128)(2,1)}, bf16[256,1...) custom-call(bf16[256,2048]{1,0:T(8,128)(2,1)} %get-tuple-element.27.r, ...), custom_call_target="tpu_custom_call" | custom-call | tf_op jit(solution)/shard_map/pallas_call | solution.py:868

commit v3 on v2

--- a/solution.py
+++ b/solution.py
@@ -14,7 +14,13 @@
 EPS = 1e-05
 SLOTS = 11 + 4 * 4
 CHUNKS = 4
-UNROLL = 4
+
+
+def chunk_bounds(nz):
+    return [0, 3, 5, 7, 8] if nz == 8 else [k * nz // CHUNKS for k in range(CHUNKS + 1)]
+
+
+WINDOW = 9
 F32 = jnp.float32
 BF = jnp.bfloat16
 MESH = pl.DeviceIdType.MESH
@@ -56,26 +62,11 @@
     ny,
     nz,
     ntp,
-    x_ref,
-    g_ref,
-    w_ref,
-    r_ref,
-    raw_ref,
-    bias_ref,
-    decay_ref,
-    skip_ref,
-    gain_ref,
-    start_ref,
-    og_ref,
-    out_ref,
-    fin_ref,
-    dx_ref,
-    dg_ref,
-    dw_ref,
-    dr_ref,
-    dstep_ref,
-    dheads_ref,
-    dnorm_ref,
+    ins,
+    outs_hbm,
+    held_in,
+    held_out,
+    io_sem,
     st_hi,
     st_mid,
     lhs_ref,
@@ -138,7 +129,24 @@
     ssem,
     rsem,
 ):
+    x_ref, g_ref, w_ref, r_ref, raw_ref, bias_ref, decay_ref, skip_ref, gain_ref = held_in[:9]
+    start_ref, og_ref = held_in[9:]
+    out_ref, fin_ref, dx_ref, dg_ref, dw_ref, dr_ref, dstep_ref, dheads_ref, dnorm_ref = held_out
     toks, cols_all = x_ref.shape
+    loads = [pltpu.make_async_copy(ins[k], held_in[k], io_sem.at[0, k]) for k in range(11)]
+    for k in (4, 5, 6, 7, 0, 2, 3, 1, 8, 9, 10):
+        loads[k].start()
+
+    def loaded(*which):
+        for k in which:
+            loads[k].wait()
+
+    stores = [pltpu.make_async_copy(held_out[k], outs_hbm[k], io_sem.at[1, k]) for k in range(9)]
+
+    def store(*which):
+        for k in which:
+            stores[k].start()
+
     heads = raw_ref.shape[0]
     pairs = heads // 2
     half = toks // 2
@@ -170,15 +178,13 @@
                 device_id_type=MESH,
             )
             partners += 1
-    pl.semaphore_wait(barrier, partners)
-
     slots = iter(range(SLOTS))
 
     def exchange(line, src, dst):
         slot = next(slots)
         count, me, where = lines[line]
         made = []
-        for d in range(1, count):
+        for d in sorted(range(1, count), key=lambda d: -min(d, count - d)):
             to = lax.rem(me + d, count)
             made.append(
                 pltpu.make_async_remote_copy(
@@ -192,10 +198,16 @@
             )
         for c in made:
             c.start()
-        started.append(lambda: [c.wait_send() for c in made])
+        started.append(made)
         return made
 
-    started = []
+    started, gone = [], []
+
+    def sent(made):
+        if not any(made is other for other in gone):
+            gone.append(made)
+            for c in made:
+                c.wait_send()
 
     def arrived(made):
         for c in made:
@@ -236,6 +248,7 @@
             jnp.where(eye, jnp.broadcast_to(col, (heads, heads)), 0.0), axis=0, keepdims=True
         )
 
+    loaded(4, 5, 6, 7)
     bias_raw = raw_ref[...] + column(bias_ref[...])
     delta = jnp.maximum(bias_raw, 0.0) + jnp.log1p(jnp.exp(-jnp.abs(bias_raw)))
     rate = jnp.exp(column(decay_ref[...]))
@@ -261,8 +274,6 @@
     for h in range(heads):
         lg_buf[h % ny, h // ny : h // ny + 1, :] = end_rows[h : h + 1, :]
     f_own[...] = jnp.exp(lg_buf[...])
-    logs_y = exchange("y", at(lg_buf), at(lg_in))
-    lg_in[0] = lg_buf[y]
 
     def put_heads(buf, j, both):
         for i in range(2):
@@ -278,14 +289,14 @@
             got.append(buf[from_y(lax.rem(h, ny)), rows, :])
         return jnp.concatenate(got, axis=0)
 
-    per_chunk = nz // CHUNKS
-
-    def loop(body, c, unroll=UNROLL):
-        n = pairs // CHUNKS
-        lax.fori_loop(c * n, (c + 1) * n, body, 0, unroll=min(n, unroll))
+    bounds = chunk_bounds(nz)
+
+    def loop(body, c):
+        lo, hi = bounds[c] * ny // 2, bounds[c + 1] * ny // 2
+        lax.fori_loop(lo, hi, body, 0, unroll=hi - lo)
 
     def chunk_rows(c):
-        return slice(c * per_chunk * P_SIZE, (c + 1) * per_chunk * P_SIZE)
+        return slice(bounds[c] * P_SIZE, bounds[c + 1] * P_SIZE)
 
     def first(j, _):
         cols = cols_of(j)
@@ -336,13 +347,15 @@
         return slice(k * P_SIZE, (k + 1) * P_SIZE)
 
     def heads_of(c):
-        return range(c * per_chunk, (c + 1) * per_chunk)
-
-    def send_y(buf, into, c):
+        return range(bounds[c], bounds[c + 1])
+
+    def send_y(buf, into, c, before):
+        if len(before) >= WINDOW:
+            sent(before[-WINDOW])
         rows = chunk_rows(c)
         made = exchange("y", at_rows(buf, rows), at_rows(into, rows))
         into[0, rows, :] = buf[y, rows, :]
-        return made
+        before.append(made)
 
     def to_owner(slot, buf, into, t):
         return pltpu.make_async_remote_copy(
@@ -392,12 +405,12 @@
                     self.into[t] = self.buf[t]
 
         def scan(self, c, body):
-            @pl.when(lax.div(z, per_chunk) == c)
+            @pl.when((z >= bounds[c]) & (z < bounds[c + 1]))
             def _():
                 for d in range(1, nz):
                     from_sender(self.there, self.buf, self.into, lax.rem(z + d, nz)).wait_recv()
                 body()
-                for d in range(1, nz):
+                for d in sorted(range(1, nz), key=lambda d: -min(d, nz - d)):
                     to_row(self.back, self.back_buf, self.back_in, d).start()
                 self.back_in[z] = self.back_buf[z]
 
@@ -443,7 +456,7 @@
                 yb_buf[k, rows_z(j), :] = state
                 if k < ny - 1:
                     state = f_ref[k, j : j + 1, :] * state + s_in[from_y(k), rows_z(j), :]
-        return send_y(yb_buf, yb_in, c)
+        send_y(yb_buf, yb_in, c, y_back)
 
     def read(j, _):
         cols = cols_of(j)
@@ -457,25 +470,31 @@
         return 0
 
     y_there, y_back = [], []
-    for c in range(CHUNKS):
+    loaded(0, 2, 3)
+    loop(first, 0)
+    pl.semaphore_wait(barrier, partners)
+    logs_y = exchange("y", at(lg_buf), at(lg_in))
+    lg_in[0] = lg_buf[y]
+    send_y(s_buf, s_in, 0, y_there)
+    for c in range(1, CHUNKS):
         loop(first, c)
-        y_there.append(send_y(s_buf, s_in, c))
-        if c == 1:
-            arrived(logs_y)
-            log_sum = jnp.zeros((8, N), F32)
-            for k in range(ny):
-                log_end = lg_in[from_y(k)]
-                f_ref[k] = jnp.exp(log_end)
-                log_sum = log_sum + log_end
-            lr_buf[...] = log_sum
-            logs_z = exchange("z", whole(lr_buf), at(lr_in))
-            lr_in[0] = log_sum
+        send_y(s_buf, s_in, c, y_there)
     causal = iota((toks, toks), 0) >= iota((toks, toks), 1)
     rwm_ref[...] = jnp.where(causal, nt(r_ref[...], w_ref[...]), 0.0)
     rwt_ref[...] = jnp.where(
         iota((toks, toks), 0) <= iota((toks, toks), 1), nt(w_ref[...], r_ref[...]), 0.0
     )
     acc_ref[...] = jnp.zeros_like(acc_ref)
+    arrived(logs_y)
+    log_sum = jnp.zeros((8, N), F32)
+    for k in range(ny):
+        log_end = lg_in[from_y(k)]
+        f_ref[k] = jnp.exp(log_end)
+        log_sum = log_sum + log_end
+    lr_buf[...] = log_sum
+    logs_z = exchange("z", whole(lr_buf), at(lr_in))
+    lr_in[0] = log_sum
+    loaded(1, 8, 9, 10)
     arrived(y_there[0])
     compose(0)
     loop(intra, 0)
@@ -494,13 +513,14 @@
     forward.scan(1, scan_forward)
     loop(intra, 3)
     forward.scan(2, scan_forward)
-    y_back.append(expand(0))
+    expand(0)
     forward.scan(3, scan_forward)
+    store(1)
     for c in range(1, 3):
-        y_back.append(expand(c))
+        expand(c)
     arrived(y_back[0])
     loop(read, 0)
-    y_back.append(expand(3))
+    expand(3)
     for c in range(1, CHUNKS):
         arrived(y_back[c])
         loop(read, c)
@@ -613,12 +633,12 @@
                 wb_buf[k, rows_z(j), :] = state
                 if k > 0:
                     state = f_ref[k, j : j + 1, :] * state + g_in[from_y(k), rows_z(j), :]
-        return send_y(wb_buf, wb_in, c)
+        send_y(wb_buf, wb_in, c, w_back)
 
     g_there, w_back = [], []
     for c in range(CHUNKS):
         loop(back, c)
-        g_there.append(send_y(g_buf, g_in, c))
+        send_y(g_buf, g_in, c, g_there)
     loop(outs, 0)
     arrived(g_there[0])
     compose_back(0)
@@ -629,6 +649,7 @@
     arrived(g_there[2])
     compose_back(2)
     loop(outs, 3)
+    store(0, 3)
     skip_sum = row_of(jnp.sum(sk_ref[...], axis=1, keepdims=True))
     ny_buf[pairs:, :] = jnp.zeros((ny_buf.shape[0] - pairs, N), F32)
     ny_buf[pairs : pairs + 1, :heads] = skip_sum
@@ -641,18 +662,19 @@
     backward.scan(1, scan_back)
     loop(intra_back, 1)
     backward.scan(2, scan_back)
-    w_back.append(expand_back(0))
+    expand_back(0)
     loop(intra_back, 2)
     backward.scan(3, scan_back)
     for c in range(1, 3):
-        w_back.append(expand_back(c))
+        expand_back(c)
     loop(intra_back, 3)
-    w_back.append(expand_back(3))
+    expand_back(3)
 
     below = iota((toks, toks), 0) <= iota((toks, toks), 1)
     drwt = jnp.where(below, drwt_ref[...], 0.0).astype(BF)
     dr_in = tn(drwt, w_ref[...])
     dr_ref[...] = (dr_in.astype(BF).astype(F32) + dwr_ref[1].astype(BF).astype(F32)).astype(BF)
+    store(5)
     dw_in = nn(drwt, r_ref[...])
     arrived(sums_y)
     total = ny_in[0]
@@ -669,7 +691,6 @@
         held = later * inc
         later = later.astype(BF)
         state_part = nt(w_ref[...], later) * te_ref[:, cols]
-        intra_part = dxi_ref[:, cols]
         x = x_ref[:, cols].astype(F32)
         written = x * state_part
         rk_ref[1] += gather_heads(j, v_ref[:, cols] + written)
@@ -680,16 +701,24 @@
             kept = jnp.sum(held[i * P_SIZE : (i + 1) * P_SIZE], axis=0, keepdims=True)
             keep = lane_low if i == 0 else jnp.logical_not(lane_low)
             es_ref[pl.ds(h, 1), :] = factor * kept + jnp.where(keep, written, 0.0)
+        te_ref[:, cols] = state_part
+        return 0
+
+    def inputs_back(j, _):
+        cols = cols_of(j)
+        state_part = te_ref[:, cols]
+        intra_part = dxi_ref[:, cols]
         direct = (d_ref[:, cols].astype(F32) * skip_of(j)).astype(BF).astype(F32)
         joined = (intra_part.astype(BF).astype(F32) + state_part.astype(BF).astype(F32)).astype(BF)
         dx_ref[:, cols] = (joined.astype(F32) + direct).astype(BF)
-        dwr_ref[0] += nn(xs_ref[:, cols], later)
+        dwr_ref[0] += nn(xs_ref[:, cols], take_heads(wb_in, j).astype(BF))
         return 0
 
     for c in range(CHUNKS):
         arrived(w_back[c])
         loop(last, c)
-    dw_ref[...] = (dw_in.astype(BF).astype(F32) + dwr_ref[0].astype(BF).astype(F32)).astype(BF)
+        if c < CHUNKS - 2:
+            loop(inputs_back, c)
 
     k_rows = jnp.transpose(rk_ref[1])[:heads]
     d_log = jnp.transpose(rk_ref[0])[:heads] - k_rows
@@ -706,6 +735,11 @@
     ly_buf[1:2, :heads] = row_of(jnp.sum(d_inc * (-rate * dl_row[...]), axis=1, keepdims=True))
     late_y = exchange("y", whole(ly_buf), at(ly_in))
     ly_in[0] = ly_buf[...]
+    for c in range(CHUNKS - 2, CHUNKS):
+        loop(inputs_back, c)
+    store(2, 6)
+    dw_ref[...] = (dw_in.astype(BF).astype(F32) + dwr_ref[0].astype(BF).astype(F32)).astype(BF)
+    store(4)
     arrived(late_y)
     total = ly_in[0]
     for k in range(1, ny):
@@ -725,20 +759,27 @@
         dnorm_ref[0:1, j * N : (j + 1) * N] = total[j : j + 1, :] * scale
     dheads_ref[0:2, :] = late[0:2, :heads] * scale
     dheads_ref[2:3, :] = total[pairs : pairs + 1, :heads] * scale
+    store(7, 8)
     forward.sent()
     backward.sent()
-    for wait in started:
-        wait()
-
-
-def copy_kernel(*refs):
-    n = (len(refs) - 1) // 2
-    sem = refs[-1]
-    made = [pltpu.make_async_copy(refs[i], refs[n + i], sem.at[i]) for i in range(n)]
-    for c in made:
-        c.start()
-    for c in made:
-        c.wait()
+    for made in started:
+        sent(made)
+    for made in stores:
+        made.wait()
+
+
+def copy_kernel(n, *refs):
+    sources, places, held, sem = refs[:n], refs[n : 2 * n], refs[2 * n : 3 * n], refs[-1]
+    made = []
+    for i in range(n):
+        load = pltpu.make_async_copy(sources[i], held[i], sem.at[0, i])
+        load.start()
+        made.append((load, pltpu.make_async_copy(held[i], places[i], sem.at[1, i])))
+    for load, store in made:
+        load.wait()
+        store.start()
+    for _, store in made:
+        store.wait()
 
 
 def solution(mesh):
@@ -768,6 +809,7 @@
             return pltpu.VMEM(shape, dtype)
 
         scratch = [
+            pltpu.SemaphoreType.DMA((2, 11)),
             v((toks, N), bf),
             v((toks, N), bf),
             v((toks, N), bf),
@@ -830,7 +872,7 @@
             pltpu.SemaphoreType.DMA((SLOTS, 8)),
             pltpu.SemaphoreType.DMA((SLOTS, 8)),
         ]
-        vmem = pl.BlockSpec(memory_space=pltpu.VMEM)
+        anywhere = pl.BlockSpec(memory_space=pl.ANY)
         shapes = [
             jax.ShapeDtypeStruct((toks, cols), bf),
             jax.ShapeDtypeStruct((P_SIZE, N), f32),
@@ -842,16 +884,7 @@
             jax.ShapeDtypeStruct((3, heads), f32),
             jax.ShapeDtypeStruct((1, cols), f32),
         ]
-        made = pl.pallas_call(
-            functools.partial(kernel, ny, nz, ntp),
-            out_shape=shapes,
-            in_specs=[vmem] * 11,
-            out_specs=[vmem] * 9,
-            scratch_shapes=scratch,
-            compiler_params=pltpu.CompilerParams(
-                collective_id=0, has_side_effects=True, vmem_limit_bytes=60 * 2**20
-            ),
-        )(
+        operands = (
             inputs,
             gate_input,
             write_proj,
@@ -864,13 +897,29 @@
             start_state.reshape(P_SIZE, N),
             out_grad,
         )
-        anywhere = pl.BlockSpec(memory_space=pl.ANY)
+        held_in = [v(a.shape, a.dtype) for a in operands]
+        held_out = [v(a.shape, a.dtype) for a in shapes]
+
+        def whole_kernel(*refs):
+            kernel(ny, nz, ntp, refs[:11], refs[11:20], refs[20:31], refs[31:40], *refs[40:])
+
         made = pl.pallas_call(
-            copy_kernel,
+            whole_kernel,
             out_shape=shapes,
-            in_specs=[vmem] * 9,
+            in_specs=[anywhere] * 11,
             out_specs=[anywhere] * 9,
-            scratch_shapes=[pltpu.SemaphoreType.DMA((9,))],
+            scratch_shapes=held_in + held_out + scratch,
+            compiler_params=pltpu.CompilerParams(
+                collective_id=0, has_side_effects=True, vmem_limit_bytes=60 * 2**20
+            ),
+        )(*operands)
+        made = pl.pallas_call(
+            functools.partial(copy_kernel, 9),
+            out_shape=shapes,
+            in_specs=[anywhere] * 9,
+            out_specs=[anywhere] * 9,
+            scratch_shapes=[v(a.shape, a.dtype) for a in shapes]
+            + [pltpu.SemaphoreType.DMA((2, 9))],
         )(*made)
         output, final, dx, dg, dw, dr, dstep, dheads, dnorm = made
         return (

time: 107 us -> 104 us (0.972)
  Pallas kernels: 106 us -> 102 us
    pallas_call x2, Pallas kernels: 106 us -> 102 us  [the longest x1 99.2 us: on_device(): pl.pallas_call(whole_kernel, out_shape=shapes, in_specs=[anywhere] * 11,...]
where the time goes in v3:
time: 104 us; the launch traced here: 103 us
  Pallas kernels  102 us (98%)
    pallas_call x1, Pallas kernels, on_device(): pl.pallas_call(whole_kernel, out_shape=shapes, in_specs=[anywhere] * 11,...  99.2 us
    pallas_call x1, Pallas kernels, on_device(): pl.pallas_call(functools.partial(copy_kernel, 9), out_shape=shapes, in_sp...  3.1 us

profile of v3, /device:TPU:32, one launch (start us, length us, event | category | flops | bytes accessed | tf_op | source)
XLA Modules:
  0.0 103.2 jit_solution(15479059691403160588)
XLA Ops:
  0.6 99.2 %shard_map.178 = (bf16[256,2048]{1,0:T(8,128)(2,1)}, f32[64,128]{1,0:T(8,128)}, bf16[256,2048]{1,0:T(8,128)(2,1)}, bf16[256,2048]{1,0:T(8,128)(2,1)}, bf16[256,1...) custom-call(bf16[256,2048]{1,0:T(8,128)(2,1)} %refs_0_.1, ...), custom_call_target="tpu_custom_call" | custom-call | tf_op jit(solution)/shard_map/pallas_call | solution.py:906
  99.9 3.1 %shard_map.179 = (bf16[256,2048]{1,0:T(8,128)(2,1)}, f32[64,128]{1,0:T(8,128)}, bf16[256,2048]{1,0:T(8,128)(2,1)}, bf16[256,2048]{1,0:T(8,128)(2,1)}, bf16[256,1...) custom-call(bf16[256,2048]{1,0:T(8,128)(2,1)} %get-tuple-element.27.r, ...), custom_call_target="tpu_custom_call" | custom-call | tf_op jit(solution)/shard_map/pallas_call | solution.py:916

commit v4 on v3

--- a/solution.py
+++ b/solution.py
@@ -17,7 +17,7 @@
 
 
 def chunk_bounds(nz):
-    return [0, 3, 5, 7, 8] if nz == 8 else [k * nz // CHUNKS for k in range(CHUNKS + 1)]
+    return [0, 1, 4, 7, 8] if nz == 8 else [k * nz // CHUNKS for k in range(CHUNKS + 1)]
 
 
 WINDOW = 9

time: 104 us -> 106 us (1.019)
  Pallas kernels: 102 us -> 105 us
    pallas_call x1, Pallas kernels: 99.2 us -> 102 us  [on_device(): pl.pallas_call(whole_kernel, out_shape=shapes, in_specs=[anywhere] * 11,...]
where the time goes in v4:
time: 106 us; the launch traced here: 105 us
  Pallas kernels  105 us (99%)
    pallas_call x1, Pallas kernels, on_device(): pl.pallas_call(whole_kernel, out_shape=shapes, in_specs=[anywhere] * 11,...  102 us
    pallas_call x1, Pallas kernels, on_device(): pl.pallas_call(functools.partial(copy_kernel, 9), out_shape=shapes, in_sp...  3.1 us

profile of v4, /device:TPU:32, one launch (start us, length us, event | category | flops | bytes accessed | tf_op | source)
XLA Modules:
  0.0 105.5 jit_solution(12353131762971513210)
XLA Ops:
  0.6 101.6 %shard_map.178 = (bf16[256,2048]{1,0:T(8,128)(2,1)}, f32[64,128]{1,0:T(8,128)}, bf16[256,2048]{1,0:T(8,128)(2,1)}, bf16[256,2048]{1,0:T(8,128)(2,1)}, bf16[256,1...) custom-call(bf16[256,2048]{1,0:T(8,128)(2,1)} %refs_0_.1, ...), custom_call_target="tpu_custom_call" | custom-call | tf_op jit(solution)/shard_map/pallas_call | solution.py:906
  102.2 3.1 %shard_map.179 = (bf16[256,2048]{1,0:T(8,128)(2,1)}, f32[64,128]{1,0:T(8,128)}, bf16[256,2048]{1,0:T(8,128)(2,1)}, bf16[256,2048]{1,0:T(8,128)(2,1)}, bf16[256,1...) custom-call(bf16[256,2048]{1,0:T(8,128)(2,1)} %get-tuple-element.27.r, ...), custom_call_target="tpu_custom_call" | custom-call | tf_op jit(solution)/shard_map/pallas_call | solution.py:916
